TPU v7x, 256 devices: a whole 4x4x8 slice. The times are simulated.
256 devices in a mesh: seq: 8 (over x, core), tensor: 32 (over y, z).
Axes of the slice: x: 4, y: 4, z: 8, core: 2. Of those that a mesh axis runs over, the one named last changes fastest.
Arguments:
- token_ids: int32 [2, 7], replicated, may hold values from 0 to 131071
- cache_lengths: int32 [7], replicated, may hold values from 1 to 10238
- embed_table: bfloat16 [131072, 4096], P('seq', 'tensor'), may hold values from -64 to 64
- attn_gain: float32 [4096], replicated, may hold values from 0.1 to 1.9
- final_gain: float32 [4096], replicated, may hold values from 0.1 to 1.9
- w_qkv: bfloat16 [4096, 3, 4096], P(None, None, 'tensor'), may hold values from -0.09375 to 0.09375
- w_out: bfloat16 [4096, 4096], P('tensor'), may hold values from -0.09375 to 0.09375
- cache_keys: bfloat16 [7, 10240, 4096], P(None, 'seq', 'tensor'), may hold values from -300 to 300
- cache_values: bfloat16 [7, 10240, 4096], P(None, 'seq', 'tensor'), may hold values from -24 to 24
Outputs:
- hidden: bfloat16 [2, 7, 4096], P(None, None, 'tensor')
- new_kv: bfloat16 [2, 2, 7, 4096], P(None, None, None, 'tensor')
- logprobs: float32 [2, 7, 131072], P(None, None, ('seq', 'tensor'))
All inputs are finite; a program needn't handle non-finite values.
Results may differ from a plain program's by a relative error of at most 0.0085.
The roundings to bfloat16 on the way count: a program that leaves them out, or rounds other values in their place, can miss the bound.
Values may be sent and summed in bfloat16 or wider, within the bound.
No kernel may reach another device: no remote copies, remote signals or barrier semaphores. Data moves between devices by JAX's collectives and lax.ppermute only.
A program may use at most 64 MiB of HBM per device.

v0:
```python
import math

import jax
import jax.numpy as jnp
from jax import lax
from jax.sharding import Mesh
from jax.sharding import PartitionSpec as P

HD = 128
SEQ = ("seq_0", "seq_1")
TENSOR = ("tensor_0", "tensor_1")
SEQ_TENSOR = ("seq_0", "seq_1", "tensor_0", "tensor_1")


epsilon = 1e-05
logit_gain = 2.0


def from_everyone(value, axis):
    copies = jnp.broadcast_to(value, (lax.axis_size(axis), *value.shape))
    return lax.all_to_all(copies, axis, split_axis=0, concat_axis=0, tiled=True)


def of_everyone(value, axis):
    everything = from_everyone(value, axis)
    return jnp.sum(everything.astype(jnp.float32), axis=0)


def in_order(parts, dim):
    parts = jnp.moveaxis(parts, 0, dim)
    shape = parts.shape
    return parts.reshape(*shape[:dim], shape[dim] * shape[dim + 1], *shape[dim + 2 :])


def gather_directly(value, axis, dim):
    parts = from_everyone(value, axis)
    return in_order(parts, dim)


def gathered_once(value, axis):
    leaves = jax.tree.leaves(value)
    sequence = sorted(range(len(leaves)), key=lambda k: -leaves[k].size)
    width = (1, *leaves[sequence[0]].shape)[-1]
    lines = [
        jnp.pad(leaves[k].reshape(-1), (0, -leaves[k].size % width)).reshape(-1, width)
        for k in sequence
    ]
    both, at, found = (from_everyone(jnp.concatenate(lines), axis), 0, {})
    for k, line in zip(sequence, lines):
        share = both[:, at : at + len(line)].reshape(len(both), -1)
        found[k] = share[:, : leaves[k].size].reshape(-1, *leaves[k].shape)
        at += len(line)
    numbers = iter(range(len(leaves)))
    return jax.tree.map(lambda _: found[next(numbers)], value)


def folded_in_pairs(pieces, combine):
    while len(jax.tree.leaves(pieces)[0]) > 1:
        pieces = jax.vmap(combine)(
            *(jax.tree.map(lambda part: part[side::2], pieces) for side in (0, 1))
        )
    return jax.tree.map(lambda part: part[0], pieces)


def combined_all(value, axis, combine):
    pieces = gathered_once(value, axis)
    return folded_in_pairs(pieces, combine)


def split_up(value, dim, count):
    shape = value.shape
    parts = value.reshape(*shape[:dim], count, shape[dim] // count, *shape[dim + 1 :])
    return jnp.moveaxis(parts, dim, 0)


def summed_on_arrival(value, axis, dim):
    parts = split_up(value, dim, lax.axis_size(axis))
    arrived = lax.all_to_all(parts, axis, split_axis=0, concat_axis=0, tiled=True)
    return arrived.sum(axis=0)


def over_copies(value, axis):
    return from_everyone(value, axis).sum(axis=0)


def collected_together(value, axis):
    leaves = jax.tree.leaves(value)
    sequence = sorted(range(len(leaves)), key=lambda k: -leaves[k].size)
    width = (1, *leaves[sequence[0]].shape)[-1]
    lines = [
        jnp.pad(leaves[k].reshape(-1), (0, -leaves[k].size % width)).reshape(-1, width)
        for k in sequence
    ]
    both, at, found = (lax.all_gather(jnp.concatenate(lines), axis), 0, {})
    for k, line in zip(sequence, lines):
        share = both[:, at : at + len(line)].reshape(len(both), -1)
        found[k] = share[:, : leaves[k].size].reshape(-1, *leaves[k].shape)
        at += len(line)
    numbers = iter(range(len(leaves)))
    return jax.tree.map(lambda _: found[next(numbers)], value)


def merged_by_axis(value, axes, combine):
    for axis in axes:
        pieces = collected_together(value, axis)
        value = jax.tree.map(lambda part: part[0], pieces)
        for k in range(1, lax.axis_size(axis)):
            value = combine(value, jax.tree.map(lambda part: part[k], pieces))
    return value


def rotate(vector, positions):
    half_size = vector.shape[-1] // 2
    frequency = 10000.0 ** (-(jnp.arange(half_size, dtype=jnp.float32) * 2.0 / vector.shape[-1]))
    angles = positions.astype(jnp.float32)[..., None] * frequency
    cosine_term = jnp.cos(angles)[:, :, None, :]
    sine_term = jnp.sin(angles)[:, :, None, :]
    first_half = vector[..., :half_size]
    second_half = vector[..., half_size:]
    return jnp.concatenate(
        [
            first_half * cosine_term - second_half * sine_term,
            first_half * sine_term + second_half * cosine_term,
        ],
        -1,
    )


def joint(earlier, later):
    earlier_max, earlier_sum, earlier_out = earlier
    later_max, later_sum, later_out = later
    highest = jnp.maximum(earlier_max, later_max)
    earlier_scale = jnp.exp(earlier_max - highest)
    later_scale = jnp.exp(later_max - highest)
    return (
        highest,
        earlier_sum * earlier_scale + later_sum * later_scale,
        earlier_out * earlier_scale[..., None] + later_out * later_scale[..., None],
    )


def pair_join(earlier, later):
    highest = jnp.maximum(earlier[0], later[0])
    return (
        highest,
        earlier[1] * jnp.exp(earlier[0] - highest) + later[1] * jnp.exp(later[0] - highest),
    )


def body(
    token_ids,
    cache_lengths,
    embed_table,
    attn_gain,
    final_gain,
    w_qkv,
    w_out,
    cache_keys,
    cache_values,
):
    streams = token_ids.shape[1]
    vocab_rows, local_width = embed_table.shape
    model_width = attn_gain.shape[0]
    heads_here = local_width // HD
    slot_count = cache_keys.shape[1]
    seq_index = lax.axis_index(SEQ)
    tensor_index = lax.axis_index(TENSOR)
    local_ids = token_ids - seq_index * vocab_rows
    inside = (local_ids >= 0) & (local_ids < vocab_rows)
    picked = embed_table[jnp.clip(local_ids, 0, vocab_rows - 1)]
    picked = jnp.where(inside[..., None], picked, jnp.zeros_like(picked))
    embed_local = of_everyone(picked.astype(jnp.float32).astype(jnp.bfloat16), SEQ).astype(
        jnp.float32
    )
    embed_whole = gather_directly(embed_local.astype(jnp.bfloat16), TENSOR, 2).astype(jnp.float32)
    normed = (
        embed_whole
        * lax.rsqrt(jnp.mean(embed_whole * embed_whole, -1, keepdims=True) + epsilon)
        * attn_gain
    ).astype(jnp.bfloat16)
    projected = jnp.einsum("sbd,dcf->sbcf", normed, w_qkv, preferred_element_type=jnp.float32)
    head_shape = (2, streams, heads_here, HD)
    positions = cache_lengths[None, :] + jnp.arange(2, dtype=jnp.int32)[:, None]
    queries = rotate(projected[:, :, 0].reshape(head_shape), positions).astype(jnp.bfloat16)
    new_keys = rotate(projected[:, :, 1].reshape(head_shape), positions).astype(jnp.bfloat16)
    new_values = projected[:, :, 2].reshape(head_shape).astype(jnp.bfloat16)
    new_kv = jnp.stack(
        [new_keys.reshape(2, streams, local_width), new_values.reshape(2, streams, local_width)]
    )
    inverse = HD ** (-0.5)
    key_rows = cache_keys.reshape(streams, slot_count, heads_here, HD)
    value_rows = cache_values.reshape(streams, slot_count, heads_here, HD)
    scores = (
        jnp.einsum("sbhe,bjhe->sbhj", queries, key_rows, preferred_element_type=jnp.float32)
        * inverse
    )
    slot_positions = seq_index * slot_count + jnp.arange(slot_count, dtype=jnp.int32)
    visible = (slot_positions[None, :] < cache_lengths[:, None])[None, :, None, :]
    local_max = jnp.max(jnp.where(visible, scores, -1e30), -1)
    weights = jnp.where(visible, jnp.exp(scores - local_max[..., None]), 0.0)
    local_sum = jnp.sum(weights, -1)
    local_out = jnp.einsum(
        "sbhj,bjhe->sbhe",
        weights,
        value_rows,
        preferred_element_type=jnp.float32,
        precision=lax.Precision.HIGHEST,
    )
    highest, cache_total, cache_out = combined_all((local_max, local_sum, local_out), SEQ, joint)
    fresh_scores = (
        jnp.einsum("sbhe,tbhe->sbht", queries, new_keys, preferred_element_type=jnp.float32)
        * inverse
    )
    allowed = (jnp.arange(2)[None, :] <= jnp.arange(2)[:, None])[:, None, None, :]
    fresh_max = jnp.max(jnp.where(allowed, fresh_scores, -1e30), -1)
    overall = jnp.maximum(highest, fresh_max)
    fresh_weights = jnp.where(allowed, jnp.exp(fresh_scores - overall[..., None]), 0.0)
    cache_scale = jnp.exp(highest - overall)
    denominator = cache_total * cache_scale + jnp.sum(fresh_weights, -1)
    numerator = cache_out * cache_scale[..., None] + jnp.einsum(
        "sbht,tbhe->sbhe",
        fresh_weights,
        new_values,
        preferred_element_type=jnp.float32,
        precision=lax.Precision.HIGHEST,
    )
    attended = (
        (numerator / denominator[..., None]).astype(jnp.bfloat16).reshape(2 * streams, local_width)
    )
    mixed_rows = jnp.dot(attended, w_out, preferred_element_type=jnp.float32).reshape(
        2, streams, model_width
    )
    mixed_local = summed_on_arrival(mixed_rows, TENSOR, 2)
    hidden = (embed_local + mixed_local).astype(jnp.bfloat16)
    hidden_float = hidden.astype(jnp.float32)
    final_squares = over_copies(jnp.sum(hidden_float * hidden_float, -1), TENSOR)
    factor_rows = (
        lax.rsqrt(final_squares / model_width + epsilon) * (logit_gain / math.sqrt(model_width))
    ).reshape(2 * streams, 1)
    final_local = lax.dynamic_slice_in_dim(final_gain, tensor_index * local_width, local_width)
    gated_rows = (hidden_float * final_local).astype(jnp.bfloat16).reshape(2 * streams, local_width)
    partial_logits = lax.dot_general(
        gated_rows, embed_table, (((1,), (1,)), ((), ())), preferred_element_type=jnp.float32
    )
    shares = summed_on_arrival(partial_logits, TENSOR, 1) * factor_rows
    share_max = jnp.max(shares, -1)
    share_sum = jnp.sum(jnp.exp(shares - share_max[:, None]), -1)
    vocab_max, vocab_sum = merged_by_axis((share_max, share_sum), SEQ_TENSOR, pair_join)
    logprobs = shares - (vocab_max + jnp.log(vocab_sum))[:, None]
    return (hidden, new_kv, logprobs.reshape(2, streams, -1))


def solution(mesh):
    split = Mesh(mesh.devices.reshape(4, 2, 4, 8), ("seq_0", "seq_1", "tensor_0", "tensor_1"))
    placed = (
        P(),
        P(),
        P(SEQ, TENSOR),
        P(),
        P(),
        P(None, None, TENSOR),
        P(TENSOR, None),
        P(None, SEQ, TENSOR),
        P(None, SEQ, TENSOR),
    )
    return jax.shard_map(
        body,
        mesh=split,
        in_specs=placed,
        out_specs=(P(None, None, TENSOR), P(None, None, None, TENSOR), P(None, None, SEQ_TENSOR)),
        check_vma=False,
    )
```

profile of v0, /device:TPU:2, one launch (start us, length us, event | category | flops | bytes accessed | tf_op | source)
XLA Modules:
  0.0 161.2 jit_solution(5824532388312060795)
XLA Ops:
  0.7 0.8 compare_and_fusion
  1.5 0.8 compare_select_fusion
  2.4 3.3 %gather_fusion = bf16[14,128]{1,0:T(8,128)(2,1)S(1)} fusion(bf16[16384,128]{1,0:T(8,128)(2,1)} %param.11, s32[1024]{0:T(1024)S(1)} %pad_clamp_fusion), kind=kCustom, calls=%fused_computation | custom fusion | bytes 7224 | tf_op jit(solution)/shard_map/gather | solution.py:170
  5.8 0.6 broadcast_in_dim.99
  6.4 5.5 %all-to-all-start = ((bf16[8,2,7,128]{3,1,2,0:T(2,128)(2,1)}), bf16[8,2,7,128]{3,1,2,0:T(2,128)(2,1)S(1)}, u32[]{:S(2)}, u32[]{:S(2)}) async-start(bf16[8,2,7,128]{3,1,2,0:T(2,128)(2,1)} %broadcast_in_dim.99), calls=%async_computation | async-start | bytes 57344 | tf_op jit(solution)/shard_map/all_to_all | solution.py:21
  11.9 0.7 broadcast_compare_fusion
  12.7 2.3 %copy.320 = bf16[4096,128]{1,0:T(8,128)(2,1)} copy(bf16[4096,128]{0,1:T(8,128)(2,1)} %bitcast.343) | data formatting | bytes 2097152 | tf_op jit(solution)/shard_map/dot_general | solution.py:230
  15.0 1.0 all-to-all-done
  16.0 0.7 broadcast_in_dim.101
  16.7 10.8 %all-to-all-start.1 = ((bf16[32,2,7,128]{3,1,2,0:T(2,128)(2,1)}), bf16[32,2,7,128]{3,1,2,0:T(2,128)(2,1)S(1)}, u32[]{:S(2)}, u32[]{:S(2)}) async-start(bf16[32,2,7,128]{3,1,2,0:T(2,128)(2,1)} %broadcast_in_dim.101), calls=%async_computation.1 | async-start | bytes 229376 | tf_op jit(solution)/shard_map/all_to_all | solution.py:21
  27.5 0.7 add_convert_fusion.1
  28.1 9.5 %all-to-all-done.1 = bf16[32,2,7,128]{3,1,2,0:T(2,128)(2,1)S(1)} async-done(((bf16[32,2,7,128]{3,1,2,0:T(2,128)(2,1)}), bf16[32,2,7,128]{3,1,2,0:T(2,128)(2,1)S(1)}, u32[]{:S(2)}, u32[]{:S(2)}) %all-to-all-start.1) | async-done | bytes 114720 | tf_op jit(solution)/shard_map/all_to_all | solution.py:21
  37.7 0.1 fusion.7
  37.8 0.1 copy.321
  37.9 0.7 convert_bitcast_fusion
  38.6 1.0 reshape.1070
  39.6 0.3 fusion.11
  39.9 0.6 fusion
  40.6 0.1 fusion.38
  40.8 0.1 convolution_multiply_fusion.1
  41.0 0.1 copy.293
  41.1 2.4 %select_reduce_fusion = (f32[2,7]{0,1:T(8,128)S(1)}, f32[2,7,1,1280]{3,0,1,2:T(2,128)S(1)}) fusion(pred[7,1280]{1,0:T(8,128)(4,1)S(1)} %broadcast_compare_fusion, bf16[7,1280,128]{2,1,0:T(8,128)(2,1)} %param.16, bf16[2,7,128]{2,1,0:T(8,128)(2,1)S(1)} %pad_maximum_fusion.2), kind=kOutput, calls=%fused_computation.24 | convolution fusion | flops 4641266 | bytes 2378040 | tf_op jit(solution)/shard_map/sbhe,bjhe->sbhj/dot_general | solution.py:194
  43.5 0.1 copy.278
  43.7 0.2 fusion.14
  43.9 2.7 %convolution_bitcast_fusion.3 = f32[2,7,1,128]{3,0,1,2:T(2,128)S(1)} fusion(bf16[7,1280,128]{2,1,0:T(8,128)(2,1)} %param.17, f32[2,7,1,1280]{3,0,1,2:T(2,128)S(1)} %get-tuple-element.74, pred[7,1280]{1,0:T(8,128)(4,1)S(1)} %broadcast_compare_fusion, f32[2,7]{0,1:T(8,128)S(1)} %get-tuple-element.73), kind=kOutput, calls=%fused_computation.8 | convolution fusion | flops 27560960 | bytes 2381624 | tf_op jit(solution)/shard_map/sbhj,bjhe->sbhe/dot_general | solution.py:202
  46.6 0.1 copy.279
  46.8 0.6 broadcast_in_dim.104
  47.5 4.7 %all-to-all-start.2 = ((f32[8,16,128]{2,1,0:T(8,128)}), f32[8,16,128]{2,1,0:T(8,128)S(1)}, u32[]{:S(2)}, u32[]{:S(2)}) async-start(f32[8,16,128]{2,1,0:T(8,128)} %broadcast_in_dim.104), calls=%async_computation.2 | async-start | bytes 131072 | tf_op jit(solution)/shard_map/all_to_all | solution.py:21
  52.3 4.1 %all-to-all-done.2 = f32[8,16,128]{2,1,0:T(8,128)S(1)} async-done(((f32[8,16,128]{2,1,0:T(8,128)}), f32[8,16,128]{2,1,0:T(8,128)S(1)}, u32[]{:S(2)}, u32[]{:S(2)}) %all-to-all-start.2) | async-done | bytes 65568 | tf_op jit(solution)/shard_map/all_to_all | solution.py:21
  56.7 0.3 slice.288
  57.0 0.3 slice.293
  57.5 0.1 copy.298
  57.6 0.1 copy.294
  57.9 0.1 copy.285
  58.0 0.1 copy.297
  58.1 0.1 copy.286
  58.2 0.1 copy.282
  58.3 0.1 copy.284
  58.4 0.1 fusion.13
  58.5 0.1 multiply_add_fusion
  58.6 0.2 fusion.6
  58.8 1.6 convolution_bitcast_fusion.1
  60.4 0.9 copy.301
  61.3 3.9 %all-to-all-start.3 = ((f32[32,2,7,128]{3,1,2,0:T(2,128)}), f32[32,2,7,128]{3,1,2,0:T(2,128)S(1)}, u32[]{:S(2)}, u32[]{:S(2)}) async-start(f32[32,2,7,128]{3,1,2,0:T(2,128)} %copy.301), calls=%async_computation.3 | async-start | bytes 458752 | tf_op jit(solution)/shard_map/all_to_all | solution.py:78
  65.1 0.8 dynamic_slice.3
  65.9 11.3 %all-to-all-done.3 = f32[32,2,7,128]{3,1,2,0:T(2,128)S(1)} async-done(((f32[32,2,7,128]{3,1,2,0:T(2,128)}), f32[32,2,7,128]{3,1,2,0:T(2,128)S(1)}, u32[]{:S(2)}, u32[]{:S(2)}) %all-to-all-start.3) | async-done | bytes 229408 | tf_op jit(solution)/shard_map/all_to_all | solution.py:78
  77.4 0.1 copy.305
  77.6 0.6 broadcast_in_dim.108
  78.2 4.2 %all-to-all-start.5 = ((f32[32,2,7]{2,1,0:T(2,128)}), f32[32,2,7]{2,1,0:T(2,128)S(1)}, u32[]{:S(2)}, u32[]{:S(2)}) async-start(f32[32,2,7]{2,1,0:T(2,128)} %broadcast_in_dim.108), calls=%async_computation.5 | async-start | bytes 65536 | tf_op jit(solution)/shard_map/all_to_all | solution.py:21
  82.4 4.4 %convolution_bitcast_fusion = f32[32,14,512]{2,1,0:T(8,128)} fusion(bf16[14,128,1]{1,0,2:T(8,128)(2,1)S(1)} %reshape.1069, bf16[32,512,128]{2,1,0:T(8,128)(2,1)} %bitcast.341), kind=kOutput, calls=%fused_computation.5 | convolution fusion | flops 58720256 | bytes 5115392 | tf_op jit(solution)/shard_map/dot_general | solution.py:242
  86.8 5.5 %all-to-all-done.5 = f32[32,2,7]{2,1,0:T(2,128)S(1)} async-done(((f32[32,2,7]{2,1,0:T(2,128)}), f32[32,2,7]{2,1,0:T(2,128)S(1)}, u32[]{:S(2)}, u32[]{:S(2)}) %all-to-all-start.5) | async-done | bytes 1824 | tf_op jit(solution)/shard_map/all_to_all | solution.py:21
  92.2 4.7 %all-to-all-start.4 = ((f32[32,14,512]{2,1,0:T(8,128)}), f32[32,14,512]{2,1,0:T(8,128)}, u32[]{:S(2)}, u32[]{:S(2)}) async-start(f32[32,14,512]{2,1,0:T(8,128)} %convolution_bitcast_fusion), calls=%async_computation.4 | async-start | bytes 2097152 | tf_op jit(solution)/shard_map/all_to_all | solution.py:78
  97.0 0.6 copy.309
  97.6 0.1 copy.323
  97.7 0.1 copy.307
  97.9 26.0 %all-to-all-done.4 = f32[32,14,512]{2,1,0:T(8,128)} async-done(((f32[32,14,512]{2,1,0:T(8,128)}), f32[32,14,512]{2,1,0:T(8,128)}, u32[]{:S(2)}, u32[]{:S(2)}) %all-to-all-start.4) | async-done | bytes 917536 | tf_op jit(solution)/shard_map/all_to_all | solution.py:78
  124.0 1.3 reduce_sum.88
  125.3 0.2 multiply_reduce_fusion
  125.5 0.2 exponential_reduce_fusion
  125.7 8.4 %all-gather.4 = f32[4,2,14]{2,1,0:T(2,128)S(1)} all-gather(f32[1,2,14]{2,1,0:T(2,128)S(1)} %maximum_bitcast_fusion), channel_id=2, replica_groups=mesh['seq_0'=4,'seq_1'=2,'tensor_0'=4,'tensor_1'=8] {'seq_0'}, dimensions={0}, use_global_device_ids=true | all-gather | bytes 560 | tf_op jit(solution)/shard_map/all_gather | solution.py:94
  134.1 1.8 %all-gather.5 = f32[2,2,14]{2,1,0:T(2,128)S(1)} all-gather(f32[1,2,14]{2,1,0:T(2,128)S(1)} %maximum_bitcast_fusion.1), channel_id=3, replica_groups=mesh['seq_0'=4,'seq_1'=2,'tensor_0'=4,'tensor_1'=8] {'seq_1'}, dimensions={0}, use_global_device_ids=true | all-gather | bytes 336 | tf_op jit(solution)/shard_map/all_gather | solution.py:94
  135.9 7.8 %all-gather.6 = f32[4,2,14]{2,1,0:T(2,128)S(1)} all-gather(f32[1,2,14]{2,1,0:T(2,128)S(1)} %maximum_bitcast_fusion.2), channel_id=4, replica_groups=mesh['seq_0'=4,'seq_1'=2,'tensor_0'=4,'tensor_1'=8] {'tensor_0'}, dimensions={0}, use_global_device_ids=true | all-gather | bytes 560 | tf_op jit(solution)/shard_map/all_gather | solution.py:94
  143.7 15.4 %all-gather.7 = f32[8,2,14]{2,1,0:T(2,128)S(1)} all-gather(f32[1,2,14]{2,1,0:T(2,128)S(1)} %maximum_bitcast_fusion.3), channel_id=5, replica_groups=mesh['seq_0'=4,'seq_1'=2,'tensor_0'=4,'tensor_1'=8] {'tensor_1'}, dimensions={0}, use_global_device_ids=true | all-gather | bytes 1008 | tf_op jit(solution)/shard_map/all_gather | solution.py:94
  160.6 0.6 copy.310
  (78 shorter events, 3.2 us)
Async XLA Ops:
  0.6 39.3 %copy-start = (bf16[4096,3,128]{2,0,1:T(8,128)(2,1)S(1)}, bf16[4096,3,128]{2,0,1:T(8,128)(2,1)}, u32[]{:S(2)}) copy-start(bf16[4096,3,128]{2,0,1:T(8,128)(2,1)} %param.14) | copy-start | bytes 9437188
  0.6 39.0 %copy-start.1 = (f32[4096]{0:T(1024)S(1)}, f32[4096]{0:T(1024)}, u32[]{:S(2)}) copy-start(f32[4096]{0:T(1024)} %param.12) | copy-start | bytes 49156
  6.4 9.5 %all-to-all-start = ((bf16[8,2,7,128]{3,1,2,0:T(2,128)(2,1)}), bf16[8,2,7,128]{3,1,2,0:T(2,128)(2,1)S(1)}, u32[]{:S(2)}, u32[]{:S(2)}) async-start(bf16[8,2,7,128]{3,1,2,0:T(2,128)(2,1)} %broadcast_in_dim.99), calls=%async_computation | async-start | bytes 57344 | tf_op jit(solution)/shard_map/all_to_all | solution.py:21
  16.7 21.0 %all-to-all-start.1 = ((bf16[32,2,7,128]{3,1,2,0:T(2,128)(2,1)}), bf16[32,2,7,128]{3,1,2,0:T(2,128)(2,1)S(1)}, u32[]{:S(2)}, u32[]{:S(2)}) async-start(bf16[32,2,7,128]{3,1,2,0:T(2,128)(2,1)} %broadcast_in_dim.101), calls=%async_computation.1 | async-start | bytes 229376 | tf_op jit(solution)/shard_map/all_to_all | solution.py:21
  47.5 8.9 %all-to-all-start.2 = ((f32[8,16,128]{2,1,0:T(8,128)}), f32[8,16,128]{2,1,0:T(8,128)S(1)}, u32[]{:S(2)}, u32[]{:S(2)}) async-start(f32[8,16,128]{2,1,0:T(8,128)} %broadcast_in_dim.104), calls=%async_computation.2 | async-start | bytes 131072 | tf_op jit(solution)/shard_map/all_to_all | solution.py:21
  61.3 16.0 %all-to-all-start.3 = ((f32[32,2,7,128]{3,1,2,0:T(2,128)}), f32[32,2,7,128]{3,1,2,0:T(2,128)S(1)}, u32[]{:S(2)}, u32[]{:S(2)}) async-start(f32[32,2,7,128]{3,1,2,0:T(2,128)} %copy.301), calls=%async_computation.3 | async-start | bytes 458752 | tf_op jit(solution)/shard_map/all_to_all | solution.py:78
  77.4 14.8 %copy-start.2 = (bf16[2,7,128]{2,0,1:T(2,128)(2,1)}, bf16[2,7,128]{2,0,1:T(2,128)(2,1)S(1)}, u32[]{:S(2)}) copy-start(bf16[2,7,128]{2,0,1:T(2,128)(2,1)S(1)} %get-tuple-element.50) | copy-start | bytes 10756
  78.2 14.1 %all-to-all-start.5 = ((f32[32,2,7]{2,1,0:T(2,128)}), f32[32,2,7]{2,1,0:T(2,128)S(1)}, u32[]{:S(2)}, u32[]{:S(2)}) async-start(f32[32,2,7]{2,1,0:T(2,128)} %broadcast_in_dim.108), calls=%async_computation.5 | async-start | bytes 65536 | tf_op jit(solution)/shard_map/all_to_all | solution.py:21
  92.2 31.7 %all-to-all-start.4 = ((f32[32,14,512]{2,1,0:T(8,128)}), f32[32,14,512]{2,1,0:T(8,128)}, u32[]{:S(2)}, u32[]{:S(2)}) async-start(f32[32,14,512]{2,1,0:T(8,128)} %convolution_bitcast_fusion), calls=%async_computation.4 | async-start | bytes 2097152 | tf_op jit(solution)/shard_map/all_to_all | solution.py:78
where the time goes:
time: 162 us; the launch traced here: 161 us
  waiting for transfers between devices  57.5 us (35%)
  starting transfers between devices  33.7 us (21%)
  blocking collectives  33.4 us (21%)
  local copies, waits for them, and re-layouts  16.2 us (10%)
  matrix products  12 us (7%)
  other arithmetic  7.5 us (5%)
    all_to_all x2, waiting for transfers between devices, summed_on_arrival(): lax.all_to_all(parts, axis, split_axis=0, concat_axis=0, tiled=True)  37.4 us
    all_gather x4, blocking collectives, collected_together(): both, at, found = (lax.all_gather(jnp.concatenate(lines), axis), 0, {})  33.4 us
    all_to_all x4, starting transfers between devices, from_everyone(): return lax.all_to_all(copies, axis, split_axis=0, concat_axis=0, tiled=True)  25.2 us
    all_to_all x4, waiting for transfers between devices, from_everyone(): return lax.all_to_all(copies, axis, split_axis=0, concat_axis=0, tiled=True)  20.1 us
    all_to_all x2, starting transfers between devices, summed_on_arrival(): lax.all_to_all(parts, axis, split_axis=0, concat_axis=0, tiled=True)  8.52 us
    dot_general x1, matrix products, body(): lax.dot_general(gated_rows, embed_table, (((1,), (1,)), ((), ())), prefer...  4.39 us
    gather x2, local copies, waits for them, and re-layouts, body(): picked = embed_table[jnp.clip(local_ids, 0, vocab_rows - 1)]  3.3 us
  transfers between devices with their start and end apart: 6, of which 6 were waited for; matrix products, arithmetic and copies ran while one was open for 6% of the time, Pallas kernels for 0%

commit v1 on v0

--- a/solution.py
+++ b/solution.py
@@ -10,6 +10,7 @@
 SEQ = ("seq_0", "seq_1")
 TENSOR = ("tensor_0", "tensor_1")
 SEQ_TENSOR = ("seq_0", "seq_1", "tensor_0", "tensor_1")
+EVERYONE = ("tensor_1", "tensor_0", "seq_0", "seq_1")
 
 
 epsilon = 1e-05
@@ -76,37 +77,7 @@
 def summed_on_arrival(value, axis, dim):
     parts = split_up(value, dim, lax.axis_size(axis))
     arrived = lax.all_to_all(parts, axis, split_axis=0, concat_axis=0, tiled=True)
-    return arrived.sum(axis=0)
-
-
-def over_copies(value, axis):
-    return from_everyone(value, axis).sum(axis=0)
-
-
-def collected_together(value, axis):
-    leaves = jax.tree.leaves(value)
-    sequence = sorted(range(len(leaves)), key=lambda k: -leaves[k].size)
-    width = (1, *leaves[sequence[0]].shape)[-1]
-    lines = [
-        jnp.pad(leaves[k].reshape(-1), (0, -leaves[k].size % width)).reshape(-1, width)
-        for k in sequence
-    ]
-    both, at, found = (lax.all_gather(jnp.concatenate(lines), axis), 0, {})
-    for k, line in zip(sequence, lines):
-        share = both[:, at : at + len(line)].reshape(len(both), -1)
-        found[k] = share[:, : leaves[k].size].reshape(-1, *leaves[k].shape)
-        at += len(line)
-    numbers = iter(range(len(leaves)))
-    return jax.tree.map(lambda _: found[next(numbers)], value)
-
-
-def merged_by_axis(value, axes, combine):
-    for axis in axes:
-        pieces = collected_together(value, axis)
-        value = jax.tree.map(lambda part: part[0], pieces)
-        for k in range(1, lax.axis_size(axis)):
-            value = combine(value, jax.tree.map(lambda part: part[k], pieces))
-    return value
+    return arrived.astype(jnp.float32).sum(axis=0)
 
 
 def rotate(vector, positions):
@@ -139,12 +110,10 @@
     )
 
 
-def pair_join(earlier, later):
-    highest = jnp.maximum(earlier[0], later[0])
-    return (
-        highest,
-        earlier[1] * jnp.exp(earlier[0] - highest) + later[1] * jnp.exp(later[0] - highest),
-    )
+def thirds(value):
+    high = lax.reduce_precision(value, 8, 7)
+    middle = lax.reduce_precision(value - high, 8, 7)
+    return jnp.concatenate([high, middle, value - high - middle]).astype(jnp.bfloat16)
 
 
 def body(
@@ -159,6 +128,7 @@
     cache_values,
 ):
     streams = token_ids.shape[1]
+    rows = 2 * streams
     vocab_rows, local_width = embed_table.shape
     model_width = attn_gain.shape[0]
     heads_here = local_width // HD
@@ -230,22 +200,36 @@
     mixed_rows = jnp.dot(attended, w_out, preferred_element_type=jnp.float32).reshape(
         2, streams, model_width
     )
-    mixed_local = summed_on_arrival(mixed_rows, TENSOR, 2)
+    mixed_local = summed_on_arrival(mixed_rows.astype(jnp.bfloat16), TENSOR, 2)
     hidden = (embed_local + mixed_local).astype(jnp.bfloat16)
     hidden_float = hidden.astype(jnp.float32)
-    final_squares = over_copies(jnp.sum(hidden_float * hidden_float, -1), TENSOR)
+    own_squares = jnp.sum(hidden_float * hidden_float, -1).reshape(rows)
+    final_local = lax.dynamic_slice_in_dim(final_gain, tensor_index * local_width, local_width)
+    gated_rows = (hidden_float * final_local).astype(jnp.bfloat16).reshape(rows, local_width)
+    partial_logits = lax.dot_general(
+        gated_rows, embed_table, (((1,), (1,)), ((), ())), preferred_element_type=jnp.float32
+    ).astype(jnp.bfloat16)
+    peers = lax.axis_size(TENSOR)
+    share_width = vocab_rows // peers
+    sent = jnp.moveaxis(partial_logits.reshape(rows, peers, share_width), 1, 0)
+    extra = jnp.pad(thirds(own_squares).reshape(1, 1, -1), ((0, 0), (0, 0), (0, share_width - 3 * rows)))
+    sent = jnp.concatenate([sent, jnp.broadcast_to(extra, (peers, 1, share_width))], 1)
+    arrived = lax.all_to_all(sent, TENSOR, split_axis=0, concat_axis=0, tiled=True)
+    summed = jnp.sum(arrived.astype(jnp.float32), axis=0)
+    final_squares = jnp.sum(summed[rows, : 3 * rows].reshape(3, rows), axis=0)
     factor_rows = (
         lax.rsqrt(final_squares / model_width + epsilon) * (logit_gain / math.sqrt(model_width))
-    ).reshape(2 * streams, 1)
-    final_local = lax.dynamic_slice_in_dim(final_gain, tensor_index * local_width, local_width)
-    gated_rows = (hidden_float * final_local).astype(jnp.bfloat16).reshape(2 * streams, local_width)
-    partial_logits = lax.dot_general(
-        gated_rows, embed_table, (((1,), (1,)), ((), ())), preferred_element_type=jnp.float32
-    )
-    shares = summed_on_arrival(partial_logits, TENSOR, 1) * factor_rows
+    ).reshape(rows, 1)
+    shares = summed[:rows] * factor_rows
     share_max = jnp.max(shares, -1)
     share_sum = jnp.sum(jnp.exp(shares - share_max[:, None]), -1)
-    vocab_max, vocab_sum = merged_by_axis((share_max, share_sum), SEQ_TENSOR, pair_join)
+    line = jnp.concatenate(
+        [jnp.pad(part, (0, 64 - rows)) for part in (share_max, share_sum)]
+    ).reshape(1, 128)
+    lines = from_everyone(line, EVERYONE)[:, 0]
+    maxima, sums = lines[:, :rows], lines[:, 64 : 64 + rows]
+    vocab_max = jnp.max(maxima, 0)
+    vocab_sum = jnp.sum(sums * jnp.exp(maxima - vocab_max), 0)
     logprobs = shares - (vocab_max + jnp.log(vocab_sum))[:, None]
     return (hidden, new_kv, logprobs.reshape(2, streams, -1))
 

time: 162 us -> 123 us (0.76)
  the two profiles are of different devices: /device:TPU:2 before, /device:TPU:1 now
where the time goes in v1:
time: 123 us; the launch traced here: 122 us
  waiting for transfers between devices  37.8 us (31%)
  starting transfers between devices  37.5 us (30%)
  blocking collectives  16.4 us (13%)
  local copies, waits for them, and re-layouts  12.1 us (10%)
  matrix products  10.9 us (9%)
  other arithmetic  6.79 us (6%)
    all_to_all x4, starting transfers between devices, from_everyone(): return lax.all_to_all(copies, axis, split_axis=0, concat_axis=0, tiled=True)  33.6 us
    all_to_all x4, waiting for transfers between devices, from_everyone(): return lax.all_to_all(copies, axis, split_axis=0, concat_axis=0, tiled=True)  29.5 us
    all_to_all x1, blocking collectives, body(): lax.all_to_all(sent, TENSOR, split_axis=0, concat_axis=0, tiled=True)  16.4 us
    all_to_all x1, waiting for transfers between devices, summed_on_arrival(): lax.all_to_all(parts, axis, split_axis=0, concat_axis=0, tiled=True)  8.35 us
    all_to_all x1, starting transfers between devices, summed_on_arrival(): lax.all_to_all(parts, axis, split_axis=0, concat_axis=0, tiled=True)  3.86 us
    dot_general x1, matrix products, body(): lax.dot_general(gated_rows, embed_table, (((1,), (1,)), ((), ())), prefer...  3.38 us
    gather x2, local copies, waits for them, and re-layouts, body(): picked = embed_table[jnp.clip(local_ids, 0, vocab_rows - 1)]  3.3 us
    dot_general x1, matrix products, body(): jnp.einsum('sbhj,bjhe->sbhe', weights, value_rows, preferred_element_type...  2.71 us
  transfers between devices with their start and end apart: 5, of which 5 were waited for; matrix products, arithmetic and copies ran while one was open for 2% of the time, Pallas kernels for 0%

profile of v1, /device:TPU:1, one launch (start us, length us, event | category | flops | bytes accessed | tf_op | source)
XLA Modules:
  0.0 122.4 jit_solution(4853677200686127428)
XLA Ops:
  0.7 0.8 compare_and_fusion
  1.5 0.8 compare_select_fusion
  2.4 3.3 %gather_fusion = bf16[14,128]{1,0:T(8,128)(2,1)S(1)} fusion(bf16[16384,128]{1,0:T(8,128)(2,1)} %param.11, s32[1024]{0:T(1024)S(1)} %pad_clamp_fusion), kind=kCustom, calls=%fused_computation | custom fusion | bytes 7224 | tf_op jit(solution)/shard_map/gather | solution.py:140
  5.8 0.6 broadcast_in_dim.107
  6.4 6.5 %all-to-all-start = ((bf16[8,2,7,128]{3,1,2,0:T(2,128)(2,1)}), bf16[8,2,7,128]{3,1,2,0:T(2,128)(2,1)S(1)}, u32[]{:S(2)}, u32[]{:S(2)}) async-start(bf16[8,2,7,128]{3,1,2,0:T(2,128)(2,1)} %broadcast_in_dim.107), calls=%async_computation | async-start | bytes 57344 | tf_op jit(solution)/shard_map/all_to_all | solution.py:22
  12.9 0.7 broadcast_compare_fusion
  13.6 4.0 %all-to-all-done = bf16[8,2,7,128]{3,1,2,0:T(2,128)(2,1)S(1)} async-done(((bf16[8,2,7,128]{3,1,2,0:T(2,128)(2,1)}), bf16[8,2,7,128]{3,1,2,0:T(2,128)(2,1)S(1)}, u32[]{:S(2)}, u32[]{:S(2)}) %all-to-all-start) | async-done | bytes 28704 | tf_op jit(solution)/shard_map/all_to_all | solution.py:22
  17.6 0.7 broadcast_in_dim.109
  18.3 10.5 %all-to-all-start.1 = ((bf16[32,2,7,128]{3,1,2,0:T(2,128)(2,1)}), bf16[32,2,7,128]{3,1,2,0:T(2,128)(2,1)S(1)}, u32[]{:S(2)}, u32[]{:S(2)}) async-start(bf16[32,2,7,128]{3,1,2,0:T(2,128)(2,1)} %broadcast_in_dim.109), calls=%async_computation.1 | async-start | bytes 229376 | tf_op jit(solution)/shard_map/all_to_all | solution.py:22
  28.9 0.7 add_convert_fusion.1
  29.5 8.4 %all-to-all-done.1 = bf16[32,2,7,128]{3,1,2,0:T(2,128)(2,1)S(1)} async-done(((bf16[32,2,7,128]{3,1,2,0:T(2,128)(2,1)}), bf16[32,2,7,128]{3,1,2,0:T(2,128)(2,1)S(1)}, u32[]{:S(2)}, u32[]{:S(2)}) %all-to-all-start.1) | async-done | bytes 114720 | tf_op jit(solution)/shard_map/all_to_all | solution.py:22
  38.0 0.2 fusion.8
  38.2 0.9 fusion.12
  39.1 0.6 fusion
  39.7 0.1 fusion.41
  40.0 0.1 convolution_multiply_fusion.1
  40.1 0.1 copy.196
  40.3 2.4 %select_reduce_fusion = (f32[2,7]{0,1:T(8,128)S(1)}, f32[2,7,1,1280]{3,0,1,2:T(2,128)S(1)}) fusion(pred[7,1280]{1,0:T(8,128)(4,1)S(1)} %broadcast_compare_fusion, bf16[7,1280,128]{2,1,0:T(8,128)(2,1)} %param.16, bf16[2,7,128]{2,1,0:T(8,128)(2,1)S(1)} %pad_maximum_fusion.3), kind=kOutput, calls=%fused_computation.29 | convolution fusion | flops 4641266 | bytes 2378040 | tf_op jit(solution)/shard_map/sbhe,bjhe->sbhj/dot_general | solution.py:164
  42.7 0.1 copy.181
  42.9 0.2 fusion.18
  43.1 2.7 %convolution_bitcast_fusion.1 = f32[2,7,1,128]{3,0,1,2:T(2,128)S(1)} fusion(bf16[7,1280,128]{2,1,0:T(8,128)(2,1)} %param.17, f32[2,7,1,1280]{3,0,1,2:T(2,128)S(1)} %get-tuple-element.49, pred[7,1280]{1,0:T(8,128)(4,1)S(1)} %broadcast_compare_fusion, f32[2,7]{0,1:T(8,128)S(1)} %get-tuple-element.48), kind=kOutput, calls=%fused_computation.8 | convolution fusion | flops 27560960 | bytes 2381624 | tf_op jit(solution)/shard_map/sbhj,bjhe->sbhe/dot_general | solution.py:172
  45.8 0.1 copy.182
  46.0 0.6 broadcast_in_dim.112
  46.7 5.4 %all-to-all-start.2 = ((f32[8,16,128]{2,1,0:T(8,128)}), f32[8,16,128]{2,1,0:T(8,128)S(1)}, u32[]{:S(2)}, u32[]{:S(2)}) async-start(f32[8,16,128]{2,1,0:T(8,128)} %broadcast_in_dim.112), calls=%async_computation.2 | async-start | bytes 131072 | tf_op jit(solution)/shard_map/all_to_all | solution.py:22
  52.1 4.8 %all-to-all-done.2 = f32[8,16,128]{2,1,0:T(8,128)S(1)} async-done(((f32[8,16,128]{2,1,0:T(8,128)}), f32[8,16,128]{2,1,0:T(8,128)S(1)}, u32[]{:S(2)}, u32[]{:S(2)}) %all-to-all-start.2) | async-done | bytes 65568 | tf_op jit(solution)/shard_map/all_to_all | solution.py:22
  57.2 0.3 slice.112
  57.5 0.3 slice.117
  58.0 0.1 copy.201
  58.1 0.1 copy.197
  58.2 0.1 copy.191
  58.3 0.1 copy.190
  58.4 0.1 copy.188
  58.5 0.1 copy.200
  58.6 0.1 copy.189
  58.7 0.1 copy.185
  58.8 0.1 copy.187
  58.9 0.1 fusion.14
  59.0 0.1 multiply_add_fusion
  59.1 0.2 fusion.6
  59.3 1.5 %convolution_convert_fusion.1 = bf16[2,7,4096]{2,1,0:T(8,128)(2,1)S(1)} fusion(bf16[128,4096]{1,0:T(8,128)(2,1)} %param.15, bf16[2,7,128]{2,0,1:T(2,128)(2,1)S(1)} %fusion.6), kind=kOutput, calls=%fused_computation.2 | convolution fusion | flops 14737408 | bytes 1166848 | tf_op jit(solution)/shard_map/dot_general | solution.py:200
  60.8 0.2 reshape.431
  61.0 0.7 copy.204
  61.7 3.9 %all-to-all-start.3 = ((bf16[32,2,7,128]{3,1,2,0:T(2,128)(2,1)}), bf16[32,2,7,128]{3,1,2,0:T(2,128)(2,1)S(1)}, u32[]{:S(2)}, u32[]{:S(2)}) async-start(bf16[32,2,7,128]{3,1,2,0:T(2,128)(2,1)} %copy.204), calls=%async_computation.3 | async-start | bytes 229376 | tf_op jit(solution)/shard_map/all_to_all | solution.py:79
  65.6 0.8 dynamic_slice.3
  66.3 8.4 %all-to-all-done.3 = bf16[32,2,7,128]{3,1,2,0:T(2,128)(2,1)S(1)} async-done(((bf16[32,2,7,128]{3,1,2,0:T(2,128)(2,1)}), bf16[32,2,7,128]{3,1,2,0:T(2,128)(2,1)S(1)}, u32[]{:S(2)}, u32[]{:S(2)}) %all-to-all-start.3) | async-done | bytes 114720 | tf_op jit(solution)/shard_map/all_to_all | solution.py:79
  74.7 0.1 convert_reduce_fusion.1
  74.9 0.1 copy.207
  75.1 3.4 %convolution_convert_fusion = bf16[14,16384]{1,0:T(8,128)(2,1)S(1)} fusion(bf16[16384,128]{1,0:T(8,128)(2,1)} %param.11, f32[14,128]{1,0:T(8,128)S(1)} %reshape.417, f32[128]{0:T(128)S(1)} %dynamic_slice.3), kind=kOutput, calls=%fused_computation.1 | convolution fusion | flops 58953216 | bytes 4660736 | tf_op jit(solution)/shard_map/dot_general | solution.py:209
  78.4 0.2 copy.226
  78.7 0.3 copy.251
  78.9 0.1 fusion.47
  79.1 0.1 pad_maximum_fusion
  79.2 16.4 %all_to_all.30 = bf16[32,15,512]{2,1,0:T(8,128)(2,1)S(1)} all-to-all(bf16[32,15,512]{2,1,0:T(8,128)(2,1)S(1)} %pad_maximum_fusion), channel_id=1, replica_groups=mesh['seq_0'=4,'seq_1'=2,'tensor_0'=4,'tensor_1'=8] {'tensor_0','tensor_1'}, dimensions={0} | all-to-all | bytes 983040 | tf_op jit(solution)/shard_map/all_to_all | solution.py:217
  95.6 0.1 convert_reduce_fusion
  95.9 0.2 fusion.16
  96.0 0.2 exponential_reduce_fusion
  96.3 0.7 broadcast_in_dim.118
  97.0 11.3 %all-to-all-start.5 = ((f32[256,1,128]{2,1,0:T(1,128)}), f32[256,1,128]{2,1,0:T(1,128)S(1)}, u32[]{:S(2)}, u32[]{:S(2)}) async-start(f32[256,1,128]{2,1,0:T(1,128)} %broadcast_in_dim.118), calls=%async_computation.5 | async-start | bytes 262144 | tf_op jit(solution)/shard_map/all_to_all | solution.py:22
  108.4 0.6 copy.209
  109.0 12.3 %all-to-all-done.5 = f32[256,1,128]{2,1,0:T(1,128)S(1)} async-done(((f32[256,1,128]{2,1,0:T(1,128)}), f32[256,1,128]{2,1,0:T(1,128)S(1)}, u32[]{:S(2)}, u32[]{:S(2)}) %all-to-all-start.5) | async-done | bytes 131104 | tf_op jit(solution)/shard_map/all_to_all | solution.py:22
  121.3 0.1 copy.208
  121.4 0.1 slice_reduce_fusion
  121.5 0.2 fusion.17
  121.8 0.6 copy.210
  (54 shorter events, 1.7 us)
Async XLA Ops:
  0.6 38.5 %copy-start = (bf16[4096,3,128]{2,0,1:T(8,128)(2,1)S(1)}, bf16[4096,3,128]{2,0,1:T(8,128)(2,1)}, u32[]{:S(2)}) copy-start(bf16[4096,3,128]{2,0,1:T(8,128)(2,1)} %param.14) | copy-start | bytes 9437188
  6.4 11.2 %all-to-all-start = ((bf16[8,2,7,128]{3,1,2,0:T(2,128)(2,1)}), bf16[8,2,7,128]{3,1,2,0:T(2,128)(2,1)S(1)}, u32[]{:S(2)}, u32[]{:S(2)}) async-start(bf16[8,2,7,128]{3,1,2,0:T(2,128)(2,1)} %broadcast_in_dim.107), calls=%async_computation | async-start | bytes 57344 | tf_op jit(solution)/shard_map/all_to_all | solution.py:22
  18.3 19.6 %all-to-all-start.1 = ((bf16[32,2,7,128]{3,1,2,0:T(2,128)(2,1)}), bf16[32,2,7,128]{3,1,2,0:T(2,128)(2,1)S(1)}, u32[]{:S(2)}, u32[]{:S(2)}) async-start(bf16[32,2,7,128]{3,1,2,0:T(2,128)(2,1)} %broadcast_in_dim.109), calls=%async_computation.1 | async-start | bytes 229376 | tf_op jit(solution)/shard_map/all_to_all | solution.py:22
  46.7 10.2 %all-to-all-start.2 = ((f32[8,16,128]{2,1,0:T(8,128)}), f32[8,16,128]{2,1,0:T(8,128)S(1)}, u32[]{:S(2)}, u32[]{:S(2)}) async-start(f32[8,16,128]{2,1,0:T(8,128)} %broadcast_in_dim.112), calls=%async_computation.2 | async-start | bytes 131072 | tf_op jit(solution)/shard_map/all_to_all | solution.py:22
  61.7 13.0 %all-to-all-start.3 = ((bf16[32,2,7,128]{3,1,2,0:T(2,128)(2,1)}), bf16[32,2,7,128]{3,1,2,0:T(2,128)(2,1)S(1)}, u32[]{:S(2)}, u32[]{:S(2)}) async-start(bf16[32,2,7,128]{3,1,2,0:T(2,128)(2,1)} %copy.204), calls=%async_computation.3 | async-start | bytes 229376 | tf_op jit(solution)/shard_map/all_to_all | solution.py:79
  74.9 3.8 %copy-start.1 = (bf16[2,7,128]{2,0,1:T(2,128)(2,1)}, bf16[2,7,128]{2,0,1:T(2,128)(2,1)S(1)}, u32[]{:S(2)}) copy-start(bf16[2,7,128]{2,0,1:T(2,128)(2,1)S(1)} %get-tuple-element.22) | copy-start | bytes 10756
  97.0 24.2 %all-to-all-start.5 = ((f32[256,1,128]{2,1,0:T(1,128)}), f32[256,1,128]{2,1,0:T(1,128)S(1)}, u32[]{:S(2)}, u32[]{:S(2)}) async-start(f32[256,1,128]{2,1,0:T(1,128)} %broadcast_in_dim.118), calls=%async_computation.5 | async-start | bytes 262144 | tf_op jit(solution)/shard_map/all_to_all | solution.py:22

commit v2 on v1

v2 whole, which is shorter than its diff:
```python
import functools
import math

import jax
import jax.numpy as jnp
from jax import lax
from jax.experimental import pallas as pl
from jax.experimental.pallas import tpu as pltpu
from jax.sharding import Mesh
from jax.sharding import PartitionSpec as P

HD = 128
TILE = 16
SEQ = ("seq_0", "seq_1")
TENSOR = ("tensor_0", "tensor_1")
SEQ_TENSOR = ("seq_0", "seq_1", "tensor_0", "tensor_1")
EVERYONE = ("tensor_1", "tensor_0", "seq_0", "seq_1")

epsilon = 1e-05
logit_gain = 2.0
lowest = -1e30
f32, bf16 = jnp.float32, jnp.bfloat16
VMEM = pl.BlockSpec(memory_space=pltpu.VMEM)
MIB = 1024 * 1024
PICK_GRANT = 61 * MIB
STAGE_GRANT = 49 * MIB + MIB // 2
ATTEND_GRANT = 51 * MIB + MIB // 2
HEAD_GRANT = 51 * MIB
ATTEND_CHUNKS = 8
IN_FLIGHT = 4
STAGED = 18
SMEM = pl.BlockSpec(memory_space=pltpu.SMEM)
HBM = pl.BlockSpec(memory_space=pltpu.HBM)


def exchange(copies, axis):
    return lax.all_to_all(copies, axis, split_axis=0, concat_axis=0, tiled=True)


def row_of(width=HD):
    return lax.broadcasted_iota(jnp.int32, (TILE, width), 0)


def lane_of(width=HD):
    return lax.broadcasted_iota(jnp.int32, (TILE, width), 1)


def as_line(column):
    return jnp.sum(jnp.where(row_of() == lane_of(), column, 0.0), 0, keepdims=True)


def as_column(line):
    return jnp.sum(jnp.where(row_of() == lane_of(), line, 0.0), 1, keepdims=True)


def pick_kernel(place, ids, table, out, groups, sems):
    streams = ids.shape[1]
    vocab_rows = table.shape[0]
    within, copies = [], []
    for row in range(2 * streams):
        local = ids[row // streams, row % streams] - place[0] * vocab_rows
        inside = (local >= 0) & (local < vocab_rows)
        local = jnp.clip(local, 0, vocab_rows - 1)
        offset = lax.rem(local, TILE)
        start = pl.multiple_of(local - offset, TILE)
        copy = pltpu.make_async_copy(table.at[pl.ds(start, TILE)], groups.at[row], sems.at[row])
        copy.start()
        copies.append(copy)
        within.append(jnp.where(inside, offset, TILE))
    total = jnp.zeros((TILE, HD), f32)
    for row, copy in enumerate(copies):
        copy.wait()
        block = groups[row].astype(f32)
        found = jnp.sum(jnp.where(row_of() == within[row], block, 0.0), 0, keepdims=True)
        total = jnp.where(row_of() == row, found, total)
    picked = total.astype(bf16)
    for peer in range(out.shape[0]):
        out[peer] = picked


class Stream:
    def __init__(self, copies):
        self.copies, self.begun, self.done = copies, 0, 0
        for _ in range(min(IN_FLIGHT, len(copies))):
            self.begin()

    def begin(self):
        if self.begun < len(self.copies):
            self.copies[self.begun].start()
            self.begun += 1

    def wait(self):
        self.copies[self.done].wait()
        self.done += 1
        self.begin()


def stage_kernel(after, table, out, sems):
    del after
    chunks = sems.shape[0]
    tall = out.shape[0] // chunks
    copies = [
        pltpu.make_async_copy(
            table.at[pl.ds(k * tall, tall)], out.at[pl.ds(k * tall, tall)], sems.at[k]
        )
        for k in range(chunks)
    ]
    for copy in copies:
        copy.start()
    for copy in copies:
        copy.wait()


def attend_kernel(
    place,
    lengths,
    gathered,
    gain,
    cosine,
    sine,
    keys,
    all_w_qkv,
    all_values,
    out,
    new_kv,
    w_qkv,
    values,
    weight_sems,
    value_sems,
):
    streams, slots, _ = keys.shape
    chunks = weight_sems.shape[0]
    tall = w_qkv.shape[1] // chunks
    weight_copies = [
        pltpu.make_async_copy(
            all_w_qkv.at[:, pl.ds(k * tall, tall)], w_qkv.at[:, pl.ds(k * tall, tall)], weight_sems.at[k]
        )
        for k in range(chunks)
    ]
    value_copies = [
        pltpu.make_async_copy(all_values.at[b], values.at[b], value_sems.at[b])
        for b in range(streams)
    ]
    arrivals = Stream(weight_copies + value_copies)
    blocks = gathered.shape[0]
    width = blocks * HD
    seq = place[0]
    squares = jnp.zeros((TILE, HD), f32)
    for k in range(blocks):
        part = gathered[k].astype(f32)
        squares = squares + part * part
    scale = lax.rsqrt(jnp.sum(squares, 1, keepdims=True) / width + epsilon)
    normed = [
        (gathered[k].astype(f32) * scale * gain[k : k + 1]).astype(bf16) for k in range(blocks)
    ]
    per = blocks // chunks
    projected = [jnp.zeros((TILE, HD), f32)] * 3
    for k in range(chunks):
        some = jnp.concatenate(normed[k * per : (k + 1) * per], 1)
        arrivals.wait()
        projected = [
            total
            + jnp.dot(some, w_qkv[c, k * tall : (k + 1) * tall, :], preferred_element_type=f32)
            for c, total in enumerate(projected)
        ]
    query, key, value = projected

    def rotated(part):
        return (part * cosine[...] + pltpu.roll(part, HD // 2, 1) * sine[...]).astype(bf16)

    query, key, value = rotated(query), rotated(key), value.astype(bf16)
    new_kv[0] = key
    new_kv[1] = value

    inverse = HD ** (-0.5)
    over_lanes = (((1,), (1,)), ((), ()))
    rows = row_of(slots)
    scores = jnp.zeros((TILE, slots), f32)
    length = jnp.zeros((TILE, slots), jnp.int32)
    for b in range(streams):
        mine = (rows == b) | (rows == streams + b)
        some = lax.dot_general(query, keys[b], over_lanes, preferred_element_type=f32)
        scores = jnp.where(mine, some, scores)
        length = jnp.where(mine, lengths[b], length)
    visible = lane_of(slots) + seq * slots < length
    scores = jnp.where(visible, scores * inverse, lowest)

    row, lane = row_of(TILE), lane_of(TILE)
    step, lane_step = (row >= streams).astype(jnp.int32), (lane >= streams).astype(jnp.int32)
    allowed = (row - step * streams == lane - lane_step * streams) & (lane_step <= step)
    allowed = allowed & (row < 2 * streams) & (lane < 2 * streams) & (seq == 0)
    fresh = lax.dot_general(query, key, over_lanes, preferred_element_type=f32)
    fresh = jnp.where(allowed, fresh * inverse, lowest)

    highest = jnp.maximum(jnp.max(scores, 1, keepdims=True), jnp.max(fresh, 1, keepdims=True))
    weights = jnp.where(visible, jnp.exp(scores - highest), 0.0)
    fresh_weights = jnp.where(allowed, jnp.exp(fresh - highest), 0.0)
    total = jnp.sum(weights, 1, keepdims=True) + jnp.sum(fresh_weights, 1, keepdims=True)
    mixed = jnp.dot(fresh_weights.astype(bf16), value, preferred_element_type=f32)
    for b in range(streams):
        mine = (rows == b) | (rows == streams + b)
        share = jnp.where(mine, weights, 0.0).astype(bf16)
        arrivals.wait()
        mixed = mixed + jnp.dot(share, values[b], preferred_element_type=f32)
    sent = jnp.where(row_of() == TILE - 2, as_line(highest), mixed)
    sent = jnp.where(row_of() == TILE - 1, as_line(total), sent)
    for peer in range(out.shape[0]):
        out[peer] = sent


def merge_kernel(rows, parts, w_out, out):
    count = parts.shape[0]
    peaks = [as_column(parts[k, TILE - 2 : TILE - 1, :]) for k in range(count)]
    highest = functools.reduce(jnp.maximum, peaks)
    numerator = jnp.zeros((TILE, HD), f32)
    denominator = jnp.zeros((TILE, 1), f32)
    for k in range(count):
        scale = jnp.exp(peaks[k] - highest)
        numerator = numerator + parts[k] * scale
        denominator = denominator + as_column(parts[k, TILE - 1 : TILE, :]) * scale
    real = row_of() < rows
    attended = jnp.where(real, numerator / jnp.where(real, denominator, 1.0), 0.0).astype(bf16)
    per = 8
    for group in range(out.shape[0] // per):
        some = jnp.dot(
            attended, w_out[:, group * per * HD : (group + 1) * per * HD], preferred_element_type=f32
        ).astype(bf16)
        for k in range(per):
            out[group * per + k] = some[:, k * HD : (k + 1) * HD]


def head_kernel(parts, embedded, gain, staged, whole_table, hidden_out, out, table, sems):
    peers, _, share = out.shape
    first = staged.shape[0] // share
    chunks = sems.shape[0]
    tall = table.shape[0] // chunks
    arrivals = Stream(
        [
            pltpu.make_async_copy(
                whole_table.at[pl.ds(first * share + k * tall, tall)],
                table.at[pl.ds(k * tall, tall)],
                sems.at[k],
            )
            for k in range(chunks)
        ]
    )
    mixed = jnp.zeros((TILE, HD), f32)
    for k in range(parts.shape[0]):
        mixed = mixed + parts[k].astype(f32)
    hidden = (embedded[...].astype(f32) + mixed).astype(bf16)
    hidden_out[...] = hidden
    wide = hidden.astype(f32)
    squares = as_line(jnp.sum(wide * wide, 1, keepdims=True))
    high = squares.astype(bf16).astype(f32)
    middle = (squares - high).astype(bf16).astype(f32)
    low = squares - high - middle
    line = jnp.concatenate([high, middle, low, jnp.zeros((1, share - 3 * HD), f32)], 1)
    gated = (wide * gain[...]).astype(bf16)
    spare = row_of(share) == TILE - 1
    for k in range(peers):
        source, at = (staged, k) if k < first else (table, k - first)
        if k >= first and at % (tall // share) == 0:
            arrivals.wait()
        some = lax.dot_general(
            gated,
            source[at * share : (at + 1) * share, :],
            (((1,), (1,)), ((), ())),
            preferred_element_type=f32,
        )
        out[k] = jnp.where(spare, line, some).astype(bf16)


def body(
    token_ids,
    cache_lengths,
    embed_table,
    attn_gain,
    final_gain,
    w_qkv,
    w_out,
    cache_keys,
    cache_values,
):
    streams = token_ids.shape[1]
    rows = 2 * streams
    vocab_rows, local_width = embed_table.shape
    model_width = attn_gain.shape[0]
    seqs, peers = lax.axis_size(SEQ), lax.axis_size(TENSOR)
    tensor_index = lax.axis_index(TENSOR)
    place = lax.axis_index(SEQ).astype(jnp.int32).reshape(1)
    params = pltpu.CompilerParams(vmem_limit_bytes=16 * 1024 * 1024)
    shape = jax.ShapeDtypeStruct

    picked = pl.pallas_call(
        pick_kernel,
        out_shape=shape((seqs, TILE, HD), bf16),
        in_specs=[SMEM, SMEM, HBM],
        out_specs=VMEM,
        scratch_shapes=[
            pltpu.VMEM((rows, TILE, HD), bf16),
            pltpu.SemaphoreType.DMA((rows,)),
        ],
        compiler_params=pltpu.CompilerParams(vmem_limit_bytes=PICK_GRANT),
        cost_estimate=pl.CostEstimate(flops=0, bytes_accessed=2**17, transcendentals=0),
        name="pick",
    )(place, token_ids, embed_table)
    embedded = jnp.sum(exchange(picked, SEQ).astype(f32), 0).astype(bf16)
    gathered = exchange(jnp.broadcast_to(embedded, (peers, TILE, HD)), TENSOR)

    positions = (cache_lengths[None, :] + jnp.arange(2, dtype=jnp.int32)[:, None]).reshape(rows)
    half = HD // 2
    frequency = 10000.0 ** (-(jnp.arange(half, dtype=f32) * 2.0 / HD))
    angles = positions.astype(f32)[:, None] * frequency
    cosine, sine = jnp.cos(angles), jnp.sin(angles)
    padding = ((0, TILE - rows), (0, 0))
    cosine = jnp.pad(jnp.concatenate([cosine, cosine], 1), padding)
    sine = jnp.pad(jnp.concatenate([-sine, sine], 1), padding)

    parts, new_kv = pl.pallas_call(
        attend_kernel,
        out_shape=(shape((seqs, TILE, HD), f32), shape((2, TILE, HD), bf16)),
        in_specs=[SMEM, SMEM] + [VMEM] * 5 + [HBM] * 2,
        out_specs=(VMEM, VMEM),
        scratch_shapes=[
            pltpu.VMEM((3, model_width, HD), bf16),
            pltpu.VMEM(cache_values.shape, bf16),
            pltpu.SemaphoreType.DMA((ATTEND_CHUNKS,)),
            pltpu.SemaphoreType.DMA((streams,)),
        ],
        compiler_params=pltpu.CompilerParams(vmem_limit_bytes=ATTEND_GRANT),
        name="attend",
    )(
        place,
        cache_lengths,
        gathered,
        attn_gain.reshape(peers, HD),
        cosine,
        sine,
        cache_keys,
        jnp.moveaxis(w_qkv, 1, 0),
        cache_values,
    )
    mixed = pl.pallas_call(
        functools.partial(merge_kernel, rows),
        out_shape=shape((peers, TILE, HD), bf16),
        in_specs=[VMEM, VMEM],
        out_specs=VMEM,
        compiler_params=params,
        name="merge",
    )(exchange(parts, SEQ), w_out)
    share_width = vocab_rows // peers
    staged_rows = STAGED * peers // 32 * share_width
    staged = pl.pallas_call(
        stage_kernel,
        out_shape=shape((staged_rows, HD), bf16),
        in_specs=[HBM, HBM],
        out_specs=VMEM,
        scratch_shapes=[pltpu.SemaphoreType.DMA((6,))],
        compiler_params=pltpu.CompilerParams(vmem_limit_bytes=STAGE_GRANT),
        cost_estimate=pl.CostEstimate(
            flops=0, bytes_accessed=4 * HD * staged_rows, transcendentals=0
        ),
        name="stage",
    )(mixed, embed_table)
    hidden, sent = pl.pallas_call(
        head_kernel,
        out_shape=(shape((TILE, HD), bf16), shape((peers, TILE, share_width), bf16)),
        in_specs=[VMEM] * 4 + [HBM],
        out_specs=(VMEM, VMEM),
        scratch_shapes=[
            pltpu.VMEM((vocab_rows - staged_rows, HD), bf16),
            pltpu.SemaphoreType.DMA(((vocab_rows - staged_rows) // (2 * share_width),)),
        ],
        compiler_params=pltpu.CompilerParams(vmem_limit_bytes=HEAD_GRANT),
        name="head",
    )(
        exchange(mixed, TENSOR),
        embedded,
        lax.dynamic_slice_in_dim(final_gain, tensor_index * HD, HD).reshape(1, HD),
        staged,
        embed_table,
    )
    summed = jnp.sum(exchange(sent, TENSOR).astype(f32), axis=0)
    line = summed[TILE - 1, : 3 * HD].reshape(3, HD)[:, :rows]
    final_squares = jnp.sum(line, axis=0)
    factor_rows = (
        lax.rsqrt(final_squares / model_width + epsilon) * (logit_gain / math.sqrt(model_width))
    ).reshape(rows, 1)
    shares = summed[:rows] * factor_rows
    share_max = jnp.max(shares, -1)
    share_sum = jnp.sum(jnp.exp(shares - share_max[:, None]), -1)
    line = jnp.concatenate(
        [jnp.pad(part, (0, HD // 2 - rows)) for part in (share_max, share_sum)]
    ).reshape(1, HD)
    everyone = seqs * peers
    lines = exchange(jnp.broadcast_to(line, (everyone, 1, HD)), EVERYONE)[:, 0]
    maxima, sums = lines[:, :rows], lines[:, HD // 2 : HD // 2 + rows]
    vocab_max = jnp.max(maxima, 0)
    vocab_sum = jnp.sum(sums * jnp.exp(maxima - vocab_max), 0)
    logprobs = shares - (vocab_max + jnp.log(vocab_sum))[:, None]
    return (
        hidden[:rows].reshape(2, streams, local_width),
        new_kv[:, :rows].reshape(2, 2, streams, local_width),
        logprobs.reshape(2, streams, -1),
    )


def solution(mesh):
    split = Mesh(mesh.devices.reshape(4, 2, 4, 8), ("seq_0", "seq_1", "tensor_0", "tensor_1"))
    placed = (
        P(),
        P(),
        P(SEQ, TENSOR),
        P(),
        P(),
        P(None, None, TENSOR),
        P(TENSOR, None),
        P(None, SEQ, TENSOR),
        P(None, SEQ, TENSOR),
    )
    return jax.shard_map(
        body,
        mesh=split,
        in_specs=placed,
        out_specs=(P(None, None, TENSOR), P(None, None, None, TENSOR), P(None, None, SEQ_TENSOR)),
        check_vma=False,
    )
```

time: 123 us -> 111 us (0.902)
  Pallas kernels: 0 us -> 13.7 us
  matrix products: 10.9 us -> 0 us
  blocking collectives: 16.4 us -> 27 us
  local copies, waits for them, and re-layouts: 12.1 us -> 3.51 us
  starting transfers between devices: 37.5 us -> 31.5 us
  other arithmetic: 6.79 us -> 1.19 us
  waiting for transfers between devices: 37.8 us -> 32.8 us
    pallas_call x0 -> x5, Pallas kernels: none -> 13.7 us  [the longest x1 5.89 us: body(): pl.pallas_call(attend_kernel, out_shape=(shape((seqs, TILE, HD), f32), sh...]
    dot_general x7 -> x0, matrix products: 10.9 us -> none  [the longest x1 3.38 us: body(): lax.dot_general(gated_rows, embed_table, (((1,), (1,)), ((), ())), prefer...]
    all_to_all x1 -> x2, blocking collectives: 16.4 us -> 27 us  [exchange(): return lax.all_to_all(copies, axis, split_axis=0, concat_axis=0, tiled=True)]
    all_to_all x5 -> x4, starting transfers between devices: 37.5 us -> 31.5 us  [exchange(): return lax.all_to_all(copies, axis, split_axis=0, concat_axis=0, tiled=True)]
    all_to_all x5 -> x4, waiting for transfers between devices: 37.8 us -> 32.8 us  [exchange(): return lax.all_to_all(copies, axis, split_axis=0, concat_axis=0, tiled=True)]
    gather x2 -> x0, local copies, waits for them, and re-layouts: 3.3 us -> none  [body(): picked = embed_table[jnp.clip(local_ids, 0, vocab_rows - 1)]]
    convert_element_type x3 -> x1, other arithmetic: 1.57 us -> 0.01 us  [body(): angles = positions.astype(f32)[:, None] * frequency]
    broadcast_in_dim x6 -> x2, local copies, waits for them, and re-layouts: 2.8 us -> 1.37 us  [the longest x1 0.72 us: body(): lines = exchange(jnp.broadcast_to(line, (everyone, 1, HD)), EVERYONE)[:, 0]]
  transfers between devices with their start and end apart: 5 -> 4, of which waited for: 5 -> 4; matrix products, arithmetic and copies ran while one was open for 2% -> 1% of each run, Pallas kernels for 0% -> 1%
where the time goes in v2:
time: 111 us; the launch traced here: 110 us
  waiting for transfers between devices  32.8 us (30%)
  starting transfers between devices  31.5 us (28%)
  blocking collectives  27 us (24%)
  Pallas kernels  13.7 us (12%)
  local copies, waits for them, and re-layouts  3.51 us (3%)
  other arithmetic  1.19 us (1%)
    all_to_all x4, waiting for transfers between devices, exchange(): return lax.all_to_all(copies, axis, split_axis=0, concat_axis=0, tiled=True)  32.8 us
    all_to_all x4, starting transfers between devices, exchange(): return lax.all_to_all(copies, axis, split_axis=0, concat_axis=0, tiled=True)  31.5 us
    all_to_all x2, blocking collectives, exchange(): return lax.all_to_all(copies, axis, split_axis=0, concat_axis=0, tiled=True)  27 us
    pallas_call x1, Pallas kernels, body(): pl.pallas_call(attend_kernel, out_shape=(shape((seqs, TILE, HD), f32), sh...  5.89 us
    pallas_call x1, Pallas kernels, body(): pl.pallas_call(head_kernel, out_shape=(shape((TILE, HD), bf16), shape((pe...  2.6 us
    pallas_call x1, Pallas kernels, body(): pl.pallas_call(pick_kernel, out_shape=shape((seqs, TILE, HD), bf16), in_s...  2.58 us
  transfers between devices with their start and end apart: 4, of which 4 were waited for; matrix products, arithmetic and copies ran while one was open for 1% of the time, Pallas kernels for 1%

profile of v2, /device:TPU:1, one launch (start us, length us, event | category | flops | bytes accessed | tf_op | source)
XLA Modules:
  0.0 110.5 jit_solution(4000964266837321123)
XLA Ops:
  0.6 0.0 copy-start
  0.6 0.0 copy-start.4
  0.7 0.0 copy-start.1
  0.7 0.0 copy-start.3
  0.7 2.6 %pick.1 = bf16[8,16,128]{2,1,0:T(8,128)(2,1)} custom-call(s32[1]{0:T(128)} %bitcast.place, s32[2,7]{1,0:T(2,128)} %ids.1, bf16[16384,128]{1,0:T(8,128)(2,1)} %whole_table.1), custom_call_target="tpu_custom_call" | custom-call | bytes 131072 | tf_op jit(solution)/shard_map/pick/pallas_call | solution.py:294
  3.3 6.6 %all-to-all-start = ((bf16[8,16,128]{2,1,0:T(8,128)(2,1)}), bf16[8,16,128]{2,1,0:T(8,128)(2,1)S(1)}, u32[]{:S(2)}, u32[]{:S(2)}) async-start(bf16[8,16,128]{2,1,0:T(8,128)(2,1)} %pick.1), calls=%async_computation | async-start | bytes 65536 | tf_op jit(solution)/shard_map/all_to_all | solution.py:37
  9.9 0.0 copy-done.4
  9.9 0.1 convert_element_type.22
  10.0 4.6 %all-to-all-done = bf16[8,16,128]{2,1,0:T(8,128)(2,1)S(1)} async-done(((bf16[8,16,128]{2,1,0:T(8,128)(2,1)}), bf16[8,16,128]{2,1,0:T(8,128)(2,1)S(1)}, u32[]{:S(2)}, u32[]{:S(2)}) %all-to-all-start) | async-done | bytes 32800 | tf_op jit(solution)/shard_map/all_to_all | solution.py:37
  14.7 0.7 broadcast_in_dim.4
  15.3 10.4 %all-to-all-start.1 = ((bf16[32,16,128]{2,1,0:T(8,128)(2,1)}), bf16[32,16,128]{2,1,0:T(8,128)(2,1)S(1)}, u32[]{:S(2)}, u32[]{:S(2)}) async-start(bf16[32,16,128]{2,1,0:T(8,128)(2,1)} %broadcast_in_dim.4), calls=%async_computation.1 | async-start | bytes 262144 | tf_op jit(solution)/shard_map/all_to_all | solution.py:37
  25.7 0.1 fusion.3
  25.9 0.1 select_maximum_fusion
  26.0 9.0 %all-to-all-done.1.gathered = bf16[32,16,128]{2,1,0:T(8,128)(2,1)S(1)} async-done(((bf16[32,16,128]{2,1,0:T(8,128)(2,1)}), bf16[32,16,128]{2,1,0:T(8,128)(2,1)S(1)}, u32[]{:S(2)}, u32[]{:S(2)}) %all-to-all-start.1) | async-done | bytes 131104 | tf_op jit(solution)/shard_map/all_to_all | solution.py:37
  34.9 0.0 copy-done.1
  34.9 0.0 copy-done.3
  34.9 0.0 copy-start.2
  34.9 5.9 %attend.1 = (f32[8,16,128]{2,1,0:T(8,128)S(1)}, bf16[2,16,128]{2,1,0:T(8,128)(2,1)S(1)}) custom-call(s32[1]{0:T(128)} %bitcast.place, s32[7]{0:T(128)S(1)} %copy-done.4, bf16[32,16,128]{2,1,0:T(8,128)(2,1)S(1)} %all-to-all-done.1.gathered, f32[32,128]{1,0:T(8,128)S(1)} %bitcast.10, f32[16,128]{1,0:T(8,128)S(1)} %get-tuple-element.30.cosine, ...), custom_call_target="tpu_custom_call" | custom-call | tf_op jit(solution)/shard_map/attend/pallas_call | solution.py:319
  40.8 9.4 %all_to_all.30.parts = f32[8,16,128]{2,1,0:T(8,128)S(1)} all-to-all(f32[8,16,128]{2,1,0:T(8,128)S(1)} %get-tuple-element.7), channel_id=1, replica_groups=mesh['seq_0'=4,'seq_1'=2,'tensor_0'=4,'tensor_1'=8] {'seq_0','seq_1'}, dimensions={0} | all-to-all | bytes 131072 | tf_op jit(solution)/shard_map/all_to_all | solution.py:37
  50.2 0.0 copy-done.2
  50.2 1.0 merge.1.after
  51.2 3.9 %all-to-all-start.3 = ((bf16[32,16,128]{2,1,0:T(8,128)(2,1)}), bf16[32,16,128]{2,1,0:T(8,128)(2,1)S(1)}, u32[]{:S(2)}, u32[]{:S(2)}) async-start(bf16[32,16,128]{2,1,0:T(8,128)(2,1)} %merge.1.after), calls=%async_computation.3 | async-start | bytes 262144 | tf_op jit(solution)/shard_map/all_to_all | solution.py:37
  55.0 0.0 copy-done
  55.0 0.1 dynamic-slice_bitcast_fusion.gain
  55.1 1.6 %stage.1.staged = bf16[9216,128]{1,0:T(8,128)(2,1)S(1)} custom-call(bf16[32,16,128]{2,1,0:T(8,128)(2,1)} %merge.1.after, bf16[16384,128]{1,0:T(8,128)(2,1)} %whole_table.1), custom_call_target="tpu_custom_call" | custom-call | bytes 4718592 | tf_op jit(solution)/shard_map/stage/pallas_call | solution.py:353
  56.8 7.4 %all-to-all-done.3.parts = bf16[32,16,128]{2,1,0:T(8,128)(2,1)S(1)} async-done(((bf16[32,16,128]{2,1,0:T(8,128)(2,1)}), bf16[32,16,128]{2,1,0:T(8,128)(2,1)S(1)}, u32[]{:S(2)}, u32[]{:S(2)}) %all-to-all-start.3) | async-done | bytes 131104 | tf_op jit(solution)/shard_map/all_to_all | solution.py:37
  64.2 2.6 %head.1 = (bf16[16,128]{1,0:T(8,128)(2,1)S(1)}, bf16[32,16,512]{2,1,0:T(8,128)(2,1)S(1)}) custom-call(bf16[32,16,128]{2,1,0:T(8,128)(2,1)S(1)} %all-to-all-done.3.parts, bf16[16,128]{1,0:T(8,128)(2,1)S(1)} %reduce_sum.48.embedded, f32[1,128]{1,0:T(1,128)S(1)} %dynamic-slice_bitcast_fusion.gain, bf16[9216,128]{1,0:T(8,128)(2,1)S(1)} %stage.1.staged, ...), custom_call_target="tpu_custom_call" | custom-call | tf_op jit(solution)/shard_map/head/pallas_call | solution.py:365
  66.8 17.6 %all_to_all.31 = bf16[32,16,512]{2,1,0:T(8,128)(2,1)S(1)} all-to-all(bf16[32,16,512]{2,1,0:T(8,128)(2,1)S(1)} %get-tuple-element.10), channel_id=1, replica_groups=mesh['seq_0'=4,'seq_1'=2,'tensor_0'=4,'tensor_1'=8] {'tensor_0','tensor_1'}, dimensions={0} | all-to-all | bytes 1048576 | tf_op jit(solution)/shard_map/all_to_all | solution.py:37
  84.4 0.1 convert_reduce_fusion
  84.6 0.2 fusion.1
  84.7 0.2 exponential_reduce_fusion
  84.9 0.1 fusion.4
  85.0 0.7 broadcast_in_dim.5
  85.7 10.6 %all-to-all-start.5 = ((f32[256,1,128]{2,1,0:T(1,128)}), f32[256,1,128]{2,1,0:T(1,128)S(1)}, u32[]{:S(2)}, u32[]{:S(2)}) async-start(f32[256,1,128]{2,1,0:T(1,128)} %broadcast_in_dim.5), calls=%async_computation.5 | async-start | bytes 262144 | tf_op jit(solution)/shard_map/all_to_all | solution.py:37
  96.4 0.6 copy.31
  97.0 0.6 copy.30
  97.6 11.8 %all-to-all-done.5 = f32[256,1,128]{2,1,0:T(1,128)S(1)} async-done(((f32[256,1,128]{2,1,0:T(1,128)}), f32[256,1,128]{2,1,0:T(1,128)S(1)}, u32[]{:S(2)}, u32[]{:S(2)}) %all-to-all-start.5) | async-done | bytes 131104 | tf_op jit(solution)/shard_map/all_to_all | solution.py:37
  109.3 0.1 copy.29
  109.4 0.1 slice_reduce_fusion
  109.6 0.2 fusion.2
  109.8 0.1 fusion
  109.9 0.6 copy.32
  (10 shorter events, 0.1 us)
Async XLA Ops:
  0.6 54.4 %copy-start = (f32[4096]{0:T(1024)S(1)}, f32[4096]{0:T(1024)}, u32[]{:S(2)}) copy-start(f32[4096]{0:T(1024)} %param.13) | copy-start | bytes 49156
  0.6 9.3 %copy-start.4 = (s32[7]{0:T(128)S(1)}, s32[7]{0:T(128)}, u32[]{:S(2)}) copy-start(s32[7]{0:T(128)} %lengths.1) | copy-start | bytes 88
  0.7 34.2 %copy-start.1 = (bf16[7,1280,128]{2,1,0:T(8,128)(2,1)S(1)}, bf16[7,1280,128]{2,1,0:T(8,128)(2,1)}, u32[]{:S(2)}) copy-start(bf16[7,1280,128]{2,1,0:T(8,128)(2,1)} %keys.1) | copy-start | bytes 6881284
  0.7 34.2 %copy-start.3 = (f32[4096]{0:T(1024)S(1)}, f32[4096]{0:T(1024)}, u32[]{:S(2)}) copy-start(f32[4096]{0:T(1024)} %param.12) | copy-start | bytes 49156
  3.3 11.4 %all-to-all-start = ((bf16[8,16,128]{2,1,0:T(8,128)(2,1)}), bf16[8,16,128]{2,1,0:T(8,128)(2,1)S(1)}, u32[]{:S(2)}, u32[]{:S(2)}) async-start(bf16[8,16,128]{2,1,0:T(8,128)(2,1)} %pick.1), calls=%async_computation | async-start | bytes 65536 | tf_op jit(solution)/shard_map/all_to_all | solution.py:37
  15.3 19.6 %all-to-all-start.1 = ((bf16[32,16,128]{2,1,0:T(8,128)(2,1)}), bf16[32,16,128]{2,1,0:T(8,128)(2,1)S(1)}, u32[]{:S(2)}, u32[]{:S(2)}) async-start(bf16[32,16,128]{2,1,0:T(8,128)(2,1)} %broadcast_in_dim.4), calls=%async_computation.1 | async-start | bytes 262144 | tf_op jit(solution)/shard_map/all_to_all | solution.py:37
  34.9 15.3 %copy-start.2 = (bf16[128,4096]{1,0:T(8,128)(2,1)S(1)}, bf16[128,4096]{1,0:T(8,128)(2,1)}, u32[]{:S(2)}) copy-start(bf16[128,4096]{1,0:T(8,128)(2,1)} %w_out.1) | copy-start | bytes 3145732
  51.2 13.0 %all-to-all-start.3 = ((bf16[32,16,128]{2,1,0:T(8,128)(2,1)}), bf16[32,16,128]{2,1,0:T(8,128)(2,1)S(1)}, u32[]{:S(2)}, u32[]{:S(2)}) async-start(bf16[32,16,128]{2,1,0:T(8,128)(2,1)} %merge.1.after), calls=%async_computation.3 | async-start | bytes 262144 | tf_op jit(solution)/shard_map/all_to_all | solution.py:37
  85.7 23.6 %all-to-all-start.5 = ((f32[256,1,128]{2,1,0:T(1,128)}), f32[256,1,128]{2,1,0:T(1,128)S(1)}, u32[]{:S(2)}, u32[]{:S(2)}) async-start(f32[256,1,128]{2,1,0:T(1,128)} %broadcast_in_dim.5), calls=%async_computation.5 | async-start | bytes 262144 | tf_op jit(solution)/shard_map/all_to_all | solution.py:37

commit v3 on v2

--- a/solution.py
+++ b/solution.py
@@ -24,11 +24,10 @@
 MIB = 1024 * 1024
 PICK_GRANT = 61 * MIB
 STAGE_GRANT = 49 * MIB + MIB // 2
-ATTEND_GRANT = 51 * MIB + MIB // 2
-HEAD_GRANT = 51 * MIB
-ATTEND_CHUNKS = 8
-IN_FLIGHT = 4
-STAGED = 18
+ATTEND_GRANT = 206 * MIB // 4
+HEAD_GRANT = 202 * MIB // 4
+W_STAGED = 16
+STAGED = 22
 SMEM = pl.BlockSpec(memory_space=pltpu.SMEM)
 HBM = pl.BlockSpec(memory_space=pltpu.HBM)
 
@@ -78,37 +77,34 @@
         out[peer] = picked
 
 
-class Stream:
-    def __init__(self, copies):
-        self.copies, self.begun, self.done = copies, 0, 0
-        for _ in range(min(IN_FLIGHT, len(copies))):
-            self.begin()
-
-    def begin(self):
-        if self.begun < len(self.copies):
-            self.copies[self.begun].start()
-            self.begun += 1
-
-    def wait(self):
-        self.copies[self.done].wait()
-        self.done += 1
-        self.begin()
-
-
-def stage_kernel(after, table, out, sems):
+def stage_kernel(after, source, out, sems):
     del after
+    lead = (slice(None),) * (len(source.shape) - 2)
     chunks = sems.shape[0]
-    tall = out.shape[0] // chunks
-    copies = [
-        pltpu.make_async_copy(
-            table.at[pl.ds(k * tall, tall)], out.at[pl.ds(k * tall, tall)], sems.at[k]
-        )
-        for k in range(chunks)
-    ]
-    for copy in copies:
-        copy.start()
+    tall = out.shape[-2] // chunks
+    copies = []
+    for k in range(chunks):
+        part = (*lead, pl.ds(k * tall, tall))
+        copies.append(pltpu.make_async_copy(source.at[part], out.at[part], sems.at[k]))
+        copies[-1].start()
     for copy in copies:
         copy.wait()
+
+
+def staged(after, source, rows):
+    shape = (*source.shape[:-2], rows, source.shape[-1])
+    return pl.pallas_call(
+        stage_kernel,
+        out_shape=jax.ShapeDtypeStruct(shape, source.dtype),
+        in_specs=[HBM, HBM],
+        out_specs=VMEM,
+        scratch_shapes=[pltpu.SemaphoreType.DMA((4,))],
+        compiler_params=pltpu.CompilerParams(vmem_limit_bytes=STAGE_GRANT),
+        cost_estimate=pl.CostEstimate(
+            flops=0, bytes_accessed=4 * math.prod(shape), transcendentals=0
+        ),
+        name="stage",
+    )(after, source)
 
 
 def attend_kernel(
@@ -118,30 +114,26 @@
     gain,
     cosine,
     sine,
-    keys,
+    w_start,
     all_w_qkv,
+    all_keys,
     all_values,
     out,
     new_kv,
-    w_qkv,
+    w_rest,
+    keys,
     values,
-    weight_sems,
-    value_sems,
+    sems,
 ):
     streams, slots, _ = keys.shape
-    chunks = weight_sems.shape[0]
-    tall = w_qkv.shape[1] // chunks
-    weight_copies = [
-        pltpu.make_async_copy(
-            all_w_qkv.at[:, pl.ds(k * tall, tall)], w_qkv.at[:, pl.ds(k * tall, tall)], weight_sems.at[k]
-        )
-        for k in range(chunks)
-    ]
-    value_copies = [
-        pltpu.make_async_copy(all_values.at[b], values.at[b], value_sems.at[b])
-        for b in range(streams)
-    ]
-    arrivals = Stream(weight_copies + value_copies)
+    first = w_start.shape[1]
+    weight_copy = pltpu.make_async_copy(
+        all_w_qkv.at[:, pl.ds(first, w_rest.shape[1])], w_rest, sems.at[0]
+    )
+    key_copy = pltpu.make_async_copy(all_keys, keys, sems.at[1])
+    value_copy = pltpu.make_async_copy(all_values, values, sems.at[2])
+    for copy in (weight_copy, key_copy, value_copy):
+        copy.start()
     blocks = gathered.shape[0]
     width = blocks * HD
     seq = place[0]
@@ -153,17 +145,16 @@
     normed = [
         (gathered[k].astype(f32) * scale * gain[k : k + 1]).astype(bf16) for k in range(blocks)
     ]
-    per = blocks // chunks
-    projected = [jnp.zeros((TILE, HD), f32)] * 3
-    for k in range(chunks):
-        some = jnp.concatenate(normed[k * per : (k + 1) * per], 1)
-        arrivals.wait()
-        projected = [
-            total
-            + jnp.dot(some, w_qkv[c, k * tall : (k + 1) * tall, :], preferred_element_type=f32)
-            for c, total in enumerate(projected)
-        ]
-    query, key, value = projected
+    begin = jnp.concatenate(normed[: first // HD], 1)
+    rest = jnp.concatenate(normed[first // HD :], 1)
+    query, key, value = (
+        jnp.dot(begin, w_start[c], preferred_element_type=f32) for c in range(3)
+    )
+    weight_copy.wait()
+    query, key, value = (
+        total + jnp.dot(rest, w_rest[c], preferred_element_type=f32)
+        for c, total in enumerate((query, key, value))
+    )
 
     def rotated(part):
         return (part * cosine[...] + pltpu.roll(part, HD // 2, 1) * sine[...]).astype(bf16)
@@ -176,12 +167,16 @@
     over_lanes = (((1,), (1,)), ((), ()))
     rows = row_of(slots)
     scores = jnp.zeros((TILE, slots), f32)
-    length = jnp.zeros((TILE, slots), jnp.int32)
+    length = jnp.zeros((TILE, 1), jnp.int32)
+    first_lane = row_of(1)
+    key_copy.wait()
     for b in range(streams):
         mine = (rows == b) | (rows == streams + b)
         some = lax.dot_general(query, keys[b], over_lanes, preferred_element_type=f32)
         scores = jnp.where(mine, some, scores)
-        length = jnp.where(mine, lengths[b], length)
+        length = jnp.where(
+            (first_lane == b) | (first_lane == streams + b), lengths[b], length
+        )
     visible = lane_of(slots) + seq * slots < length
     scores = jnp.where(visible, scores * inverse, lowest)
 
@@ -197,10 +192,10 @@
     fresh_weights = jnp.where(allowed, jnp.exp(fresh - highest), 0.0)
     total = jnp.sum(weights, 1, keepdims=True) + jnp.sum(fresh_weights, 1, keepdims=True)
     mixed = jnp.dot(fresh_weights.astype(bf16), value, preferred_element_type=f32)
+    value_copy.wait()
     for b in range(streams):
         mine = (rows == b) | (rows == streams + b)
         share = jnp.where(mine, weights, 0.0).astype(bf16)
-        arrivals.wait()
         mixed = mixed + jnp.dot(share, values[b], preferred_element_type=f32)
     sent = jnp.where(row_of() == TILE - 2, as_line(highest), mixed)
     sent = jnp.where(row_of() == TILE - 1, as_line(total), sent)
@@ -229,21 +224,13 @@
             out[group * per + k] = some[:, k * HD : (k + 1) * HD]
 
 
-def head_kernel(parts, embedded, gain, staged, whole_table, hidden_out, out, table, sems):
+def head_kernel(parts, embedded, gain, staged, whole_table, hidden_out, out, table, sem):
     peers, _, share = out.shape
     first = staged.shape[0] // share
-    chunks = sems.shape[0]
-    tall = table.shape[0] // chunks
-    arrivals = Stream(
-        [
-            pltpu.make_async_copy(
-                whole_table.at[pl.ds(first * share + k * tall, tall)],
-                table.at[pl.ds(k * tall, tall)],
-                sems.at[k],
-            )
-            for k in range(chunks)
-        ]
-    )
+    rest = pltpu.make_async_copy(
+        whole_table.at[pl.ds(first * share, table.shape[0])], table, sem
+    )
+    rest.start()
     mixed = jnp.zeros((TILE, HD), f32)
     for k in range(parts.shape[0]):
         mixed = mixed + parts[k].astype(f32)
@@ -259,8 +246,8 @@
     spare = row_of(share) == TILE - 1
     for k in range(peers):
         source, at = (staged, k) if k < first else (table, k - first)
-        if k >= first and at % (tall // share) == 0:
-            arrivals.wait()
+        if k == first:
+            rest.wait()
         some = lax.dot_general(
             gated,
             source[at * share : (at + 1) * share, :],
@@ -268,6 +255,36 @@
             preferred_element_type=f32,
         )
         out[k] = jnp.where(spare, line, some).astype(bf16)
+
+
+def share_kernel(model_width, parts, shares_out, lines_out):
+    total = parts[0].astype(f32)
+    for k in range(1, parts.shape[0]):
+        total = total + parts[k].astype(f32)
+    line = total[TILE - 1 :, :]
+    squares = as_column(line[:, :HD] + line[:, HD : 2 * HD] + line[:, 2 * HD : 3 * HD])
+    factor = lax.rsqrt(squares / model_width + epsilon) * (logit_gain / math.sqrt(model_width))
+    shares = total * factor
+    shares_out[...] = shares
+    highest = jnp.max(shares, 1, keepdims=True)
+    summed = jnp.sum(jnp.exp(shares - highest), 1, keepdims=True)
+    sent = as_line(highest) + pltpu.roll(as_line(summed), HD // 2, 1)
+    lines_out[...] = jnp.broadcast_to(sent.reshape(1, 1, HD), lines_out.shape)
+
+
+def finish_kernel(shares, lines, out):
+    every = lines[...]
+    highest = jnp.max(every, 0, keepdims=True)
+    scaled = pltpu.roll(every, HD // 2, 2) * jnp.exp(every - highest)
+    summed = jnp.sum(scaled, 0)
+    lane = lax.broadcasted_iota(jnp.int32, summed.shape, 1)
+    summed = jnp.where(lane < TILE, summed, 1.0)
+    total = as_column(highest[0] + jnp.log(summed))
+    logprobs = shares[...] - total
+    streams = out.shape[0]
+    for b in range(streams):
+        out[b, 0:1, :] = logprobs[b : b + 1, :]
+        out[b, 1:2, :] = logprobs[streams + b : streams + b + 1, :]
 
 
 def body(
@@ -316,16 +333,18 @@
     cosine = jnp.pad(jnp.concatenate([cosine, cosine], 1), padding)
     sine = jnp.pad(jnp.concatenate([-sine, sine], 1), padding)
 
+    w_qkv = jnp.moveaxis(w_qkv, 1, 0)
+    w_rows = model_width * W_STAGED // 32
     parts, new_kv = pl.pallas_call(
         attend_kernel,
         out_shape=(shape((seqs, TILE, HD), f32), shape((2, TILE, HD), bf16)),
-        in_specs=[SMEM, SMEM] + [VMEM] * 5 + [HBM] * 2,
+        in_specs=[SMEM, SMEM] + [VMEM] * 5 + [HBM] * 3,
         out_specs=(VMEM, VMEM),
         scratch_shapes=[
-            pltpu.VMEM((3, model_width, HD), bf16),
+            pltpu.VMEM((3, model_width - w_rows, HD), bf16),
+            pltpu.VMEM(cache_keys.shape, bf16),
             pltpu.VMEM(cache_values.shape, bf16),
-            pltpu.SemaphoreType.DMA((ATTEND_CHUNKS,)),
-            pltpu.SemaphoreType.DMA((streams,)),
+            pltpu.SemaphoreType.DMA((3,)),
         ],
         compiler_params=pltpu.CompilerParams(vmem_limit_bytes=ATTEND_GRANT),
         name="attend",
@@ -336,8 +355,9 @@
         attn_gain.reshape(peers, HD),
         cosine,
         sine,
+        staged(embedded, w_qkv, w_rows),
+        w_qkv,
         cache_keys,
-        jnp.moveaxis(w_qkv, 1, 0),
         cache_values,
     )
     mixed = pl.pallas_call(
@@ -350,18 +370,7 @@
     )(exchange(parts, SEQ), w_out)
     share_width = vocab_rows // peers
     staged_rows = STAGED * peers // 32 * share_width
-    staged = pl.pallas_call(
-        stage_kernel,
-        out_shape=shape((staged_rows, HD), bf16),
-        in_specs=[HBM, HBM],
-        out_specs=VMEM,
-        scratch_shapes=[pltpu.SemaphoreType.DMA((6,))],
-        compiler_params=pltpu.CompilerParams(vmem_limit_bytes=STAGE_GRANT),
-        cost_estimate=pl.CostEstimate(
-            flops=0, bytes_accessed=4 * HD * staged_rows, transcendentals=0
-        ),
-        name="stage",
-    )(mixed, embed_table)
+    table_start = staged(mixed, embed_table, staged_rows)
     hidden, sent = pl.pallas_call(
         head_kernel,
         out_shape=(shape((TILE, HD), bf16), shape((peers, TILE, share_width), bf16)),
@@ -369,7 +378,7 @@
         out_specs=(VMEM, VMEM),
         scratch_shapes=[
             pltpu.VMEM((vocab_rows - staged_rows, HD), bf16),
-            pltpu.SemaphoreType.DMA(((vocab_rows - staged_rows) // (2 * share_width),)),
+            pltpu.SemaphoreType.DMA,
         ],
         compiler_params=pltpu.CompilerParams(vmem_limit_bytes=HEAD_GRANT),
         name="head",
@@ -377,31 +386,30 @@
         exchange(mixed, TENSOR),
         embedded,
         lax.dynamic_slice_in_dim(final_gain, tensor_index * HD, HD).reshape(1, HD),
-        staged,
+        table_start,
         embed_table,
     )
-    summed = jnp.sum(exchange(sent, TENSOR).astype(f32), axis=0)
-    line = summed[TILE - 1, : 3 * HD].reshape(3, HD)[:, :rows]
-    final_squares = jnp.sum(line, axis=0)
-    factor_rows = (
-        lax.rsqrt(final_squares / model_width + epsilon) * (logit_gain / math.sqrt(model_width))
-    ).reshape(rows, 1)
-    shares = summed[:rows] * factor_rows
-    share_max = jnp.max(shares, -1)
-    share_sum = jnp.sum(jnp.exp(shares - share_max[:, None]), -1)
-    line = jnp.concatenate(
-        [jnp.pad(part, (0, HD // 2 - rows)) for part in (share_max, share_sum)]
-    ).reshape(1, HD)
     everyone = seqs * peers
-    lines = exchange(jnp.broadcast_to(line, (everyone, 1, HD)), EVERYONE)[:, 0]
-    maxima, sums = lines[:, :rows], lines[:, HD // 2 : HD // 2 + rows]
-    vocab_max = jnp.max(maxima, 0)
-    vocab_sum = jnp.sum(sums * jnp.exp(maxima - vocab_max), 0)
-    logprobs = shares - (vocab_max + jnp.log(vocab_sum))[:, None]
+    shares, lines = pl.pallas_call(
+        functools.partial(share_kernel, model_width),
+        out_shape=(shape((TILE, share_width), f32), shape((everyone, 1, HD), f32)),
+        in_specs=[VMEM],
+        out_specs=(VMEM, VMEM),
+        compiler_params=params,
+        name="share",
+    )(exchange(sent, TENSOR))
+    logprobs = pl.pallas_call(
+        finish_kernel,
+        out_shape=shape((streams, 2, share_width), f32),
+        in_specs=[VMEM, VMEM],
+        out_specs=VMEM,
+        compiler_params=params,
+        name="finish",
+    )(shares, exchange(lines, EVERYONE))
     return (
         hidden[:rows].reshape(2, streams, local_width),
         new_kv[:, :rows].reshape(2, 2, streams, local_width),
-        logprobs.reshape(2, streams, -1),
+        jnp.swapaxes(logprobs, 0, 1),
     )
 
 

time: 111 us -> 108 us (0.973)
  waiting for transfers between devices: 32.8 us -> 31.2 us
  local copies, waits for them, and re-layouts: 3.51 us -> 2.05 us
    pallas_call x1 -> x4, Pallas kernels: 1.64 us -> 5.33 us  [the longest x2 3.18 us: staged(): pl.pallas_call(stage_kernel, out_shape=jax.ShapeDtypeStruct(shape, source...]
    pallas_call x1, Pallas kernels: 5.89 us -> 4.04 us  [body(): pl.pallas_call(attend_kernel, out_shape=(shape((seqs, TILE, HD), f32), sh...]
    all_to_all x4, waiting for transfers between devices: 32.8 us -> 31.2 us  [exchange(): return lax.all_to_all(copies, axis, split_axis=0, concat_axis=0, tiled=True)]
  transfers between devices with their start and end apart: 4 -> 4, of which waited for: 4 -> 4; matrix products, arithmetic and copies ran while one was open for 1% -> 1% of each run, Pallas kernels for 1% -> 3%
where the time goes in v3:
time: 108 us
  starting transfers between devices  31.5 us (29%)
  waiting for transfers between devices  31.2 us (29%)
  blocking collectives  27 us (25%)
  Pallas kernels  14.8 us (14%)
  local copies, waits for them, and re-layouts  2.05 us (2%)
    all_to_all x4, starting transfers between devices, exchange(): return lax.all_to_all(copies, axis, split_axis=0, concat_axis=0, tiled=True)  31.5 us
    all_to_all x4, waiting for transfers between devices, exchange(): return lax.all_to_all(copies, axis, split_axis=0, concat_axis=0, tiled=True)  31.2 us
    all_to_all x2, blocking collectives, exchange(): return lax.all_to_all(copies, axis, split_axis=0, concat_axis=0, tiled=True)  27 us
    pallas_call x1, Pallas kernels, body(): pl.pallas_call(attend_kernel, out_shape=(shape((seqs, TILE, HD), f32), sh...  4.04 us
    pallas_call x2, Pallas kernels, staged(): pl.pallas_call(stage_kernel, out_shape=jax.ShapeDtypeStruct(shape, source...  3.18 us
    pallas_call x1, Pallas kernels, body(): pl.pallas_call(pick_kernel, out_shape=shape((seqs, TILE, HD), bf16), in_s...  2.64 us
  transfers between devices with their start and end apart: 4, of which 4 were waited for; matrix products, arithmetic and copies ran while one was open for 1% of the time, Pallas kernels for 3%

profile of v3, /device:TPU:1, one launch (start us, length us, event | category | flops | bytes accessed | tf_op | source)
XLA Modules:
  0.0 107.6 jit_solution(13460774875578443742)
XLA Ops:
  0.6 0.0 copy-start
  0.6 0.0 copy-start.3
  0.7 2.6 %pick.1 = bf16[8,16,128]{2,1,0:T(8,128)(2,1)} custom-call(s32[1]{0:T(128)} %bitcast.place, s32[2,7]{1,0:T(2,128)} %ids.1, bf16[16384,128]{1,0:T(8,128)(2,1)} %whole_table.1), custom_call_target="tpu_custom_call" | custom-call | bytes 131072 | tf_op jit(solution)/shard_map/pick/pallas_call | solution.py:311
  3.3 0.0 copy-start.2
  3.3 6.5 %all-to-all-start = ((bf16[8,16,128]{2,1,0:T(8,128)(2,1)}), bf16[8,16,128]{2,1,0:T(8,128)(2,1)S(1)}, u32[]{:S(2)}, u32[]{:S(2)}) async-start(bf16[8,16,128]{2,1,0:T(8,128)(2,1)} %pick.1), calls=%async_computation | async-start | bytes 65536 | tf_op jit(solution)/shard_map/all_to_all | solution.py:36
  9.9 0.0 copy-done.3
  9.9 0.1 convert_element_type.16
  10.0 4.6 %all-to-all-done = bf16[8,16,128]{2,1,0:T(8,128)(2,1)S(1)} async-done(((bf16[8,16,128]{2,1,0:T(8,128)(2,1)}), bf16[8,16,128]{2,1,0:T(8,128)(2,1)S(1)}, u32[]{:S(2)}, u32[]{:S(2)}) %all-to-all-start) | async-done | bytes 32800 | tf_op jit(solution)/shard_map/all_to_all | solution.py:36
  14.6 0.7 broadcast_in_dim.2
  15.3 10.5 %all-to-all-start.1 = ((bf16[32,16,128]{2,1,0:T(8,128)(2,1)}), bf16[32,16,128]{2,1,0:T(8,128)(2,1)S(1)}, u32[]{:S(2)}, u32[]{:S(2)}) async-start(bf16[32,16,128]{2,1,0:T(8,128)(2,1)} %broadcast_in_dim.2), calls=%async_computation.1 | async-start | bytes 262144 | tf_op jit(solution)/shard_map/all_to_all | solution.py:36
  25.8 0.1 fusion
  25.9 0.1 select_maximum_fusion
  26.0 1.4 %stage.2.w_start = bf16[3,2048,128]{2,1,0:T(8,128)(2,1)S(1)} custom-call(bf16[16,128]{1,0:T(8,128)(2,1)S(1)} %reduce_sum.12.after.embedded, bf16[3,4096,128]{2,1,0:T(8,128)(2,1)} %bitcast.12), custom_call_target="tpu_custom_call" | custom-call | bytes 3145728 | tf_op jit(solution)/shard_map/stage/pallas_call | solution.py:96
  27.4 7.6 %all-to-all-done.1.gathered = bf16[32,16,128]{2,1,0:T(8,128)(2,1)S(1)} async-done(((bf16[32,16,128]{2,1,0:T(8,128)(2,1)}), bf16[32,16,128]{2,1,0:T(8,128)(2,1)S(1)}, u32[]{:S(2)}, u32[]{:S(2)}) %all-to-all-start.1) | async-done | bytes 131104 | tf_op jit(solution)/shard_map/all_to_all | solution.py:36
  35.0 0.0 copy-done.2
  35.0 0.0 copy-start.1
  35.0 4.0 %attend.1 = (f32[8,16,128]{2,1,0:T(8,128)S(1)}, bf16[2,16,128]{2,1,0:T(8,128)(2,1)S(1)}) custom-call(s32[1]{0:T(128)} %bitcast.place, s32[7]{0:T(128)S(1)} %copy-done.3, bf16[32,16,128]{2,1,0:T(8,128)(2,1)S(1)} %all-to-all-done.1.gathered, f32[32,128]{1,0:T(8,128)S(1)} %bitcast.9, f32[16,128]{1,0:T(8,128)S(1)} %get-tuple-element.25.cosine, ...), custom_call_target="tpu_custom_call" | custom-call | tf_op jit(solution)/shard_map/attend/pallas_call | solution.py:338
  39.0 9.4 %all_to_all.30.parts = f32[8,16,128]{2,1,0:T(8,128)S(1)} all-to-all(f32[8,16,128]{2,1,0:T(8,128)S(1)} %get-tuple-element.9), channel_id=1, replica_groups=mesh['seq_0'=4,'seq_1'=2,'tensor_0'=4,'tensor_1'=8] {'seq_0','seq_1'}, dimensions={0} | all-to-all | bytes 131072 | tf_op jit(solution)/shard_map/all_to_all | solution.py:36
  48.4 0.0 copy-done.1
  48.4 1.0 merge.1.after
  49.4 3.9 %all-to-all-start.3 = ((bf16[32,16,128]{2,1,0:T(8,128)(2,1)}), bf16[32,16,128]{2,1,0:T(8,128)(2,1)S(1)}, u32[]{:S(2)}, u32[]{:S(2)}) async-start(bf16[32,16,128]{2,1,0:T(8,128)(2,1)} %merge.1.after), calls=%async_computation.3 | async-start | bytes 262144 | tf_op jit(solution)/shard_map/all_to_all | solution.py:36
  53.3 0.0 copy-done
  53.3 0.1 dynamic-slice_bitcast_fusion.gain
  53.3 1.8 %stage.3.staged = bf16[11264,128]{1,0:T(8,128)(2,1)S(1)} custom-call(bf16[32,16,128]{2,1,0:T(8,128)(2,1)} %merge.1.after, bf16[16384,128]{1,0:T(8,128)(2,1)} %whole_table.1), custom_call_target="tpu_custom_call" | custom-call | bytes 5767168 | tf_op jit(solution)/shard_map/stage/pallas_call | solution.py:96
  55.1 7.3 %all-to-all-done.3.parts = bf16[32,16,128]{2,1,0:T(8,128)(2,1)S(1)} async-done(((bf16[32,16,128]{2,1,0:T(8,128)(2,1)}), bf16[32,16,128]{2,1,0:T(8,128)(2,1)S(1)}, u32[]{:S(2)}, u32[]{:S(2)}) %all-to-all-start.3) | async-done | bytes 131104 | tf_op jit(solution)/shard_map/all_to_all | solution.py:36
  62.4 1.8 %head.1 = (bf16[16,128]{1,0:T(8,128)(2,1)S(1)}, bf16[32,16,512]{2,1,0:T(8,128)(2,1)S(1)}) custom-call(bf16[32,16,128]{2,1,0:T(8,128)(2,1)S(1)} %all-to-all-done.3.parts, bf16[16,128]{1,0:T(8,128)(2,1)S(1)} %reduce_sum.12.after.embedded, f32[1,128]{1,0:T(1,128)S(1)} %dynamic-slice_bitcast_fusion.gain, bf16[11264,128]{1,0:T(8,128)(2,1)S(1)} %stage.3.staged, ...), custom_call_target="tpu_custom_call" | custom-call | tf_op jit(solution)/shard_map/head/pallas_call | solution.py:374
  64.2 17.6 %all_to_all.31.parts = bf16[32,16,512]{2,1,0:T(8,128)(2,1)S(1)} all-to-all(bf16[32,16,512]{2,1,0:T(8,128)(2,1)S(1)} %get-tuple-element.12), channel_id=1, replica_groups=mesh['seq_0'=4,'seq_1'=2,'tensor_0'=4,'tensor_1'=8] {'tensor_0','tensor_1'}, dimensions={0} | all-to-all | bytes 1048576 | tf_op jit(solution)/shard_map/all_to_all | solution.py:36
  81.8 1.1 %share.1 = (f32[16,512]{1,0:T(8,128)S(1)}, f32[256,1,128]{2,1,0:T(1,128)}) custom-call(bf16[32,16,512]{2,1,0:T(8,128)(2,1)S(1)} %all_to_all.31.parts), custom_call_target="tpu_custom_call" | custom-call | tf_op jit(solution)/shard_map/share/pallas_call | solution.py:393
  82.9 10.6 %all-to-all-start.5 = ((f32[256,1,128]{2,1,0:T(1,128)}), f32[256,1,128]{2,1,0:T(1,128)S(1)}, u32[]{:S(2)}, u32[]{:S(2)}) async-start(f32[256,1,128]{2,1,0:T(1,128)} %get-tuple-element.14), calls=%async_computation.5 | async-start | bytes 262144 | tf_op jit(solution)/shard_map/all_to_all | solution.py:36
  93.6 0.6 copy.16
  94.2 0.6 copy.15
  94.8 11.8 %all-to-all-done.5.lines = f32[256,1,128]{2,1,0:T(1,128)S(1)} async-done(((f32[256,1,128]{2,1,0:T(1,128)}), f32[256,1,128]{2,1,0:T(1,128)S(1)}, u32[]{:S(2)}, u32[]{:S(2)}) %all-to-all-start.5) | async-done | bytes 131104 | tf_op jit(solution)/shard_map/all_to_all | solution.py:36
  106.5 1.1 finish.1
  (5 shorter events, 0.0 us)
Async XLA Ops:
  0.6 52.6 %copy-start = (f32[4096]{0:T(1024)S(1)}, f32[4096]{0:T(1024)}, u32[]{:S(2)}) copy-start(f32[4096]{0:T(1024)} %param.13) | copy-start | bytes 49156
  0.6 9.2 %copy-start.3 = (s32[7]{0:T(128)S(1)}, s32[7]{0:T(128)}, u32[]{:S(2)}) copy-start(s32[7]{0:T(128)} %lengths.1) | copy-start | bytes 88
  3.3 31.7 %copy-start.2 = (f32[4096]{0:T(1024)S(1)}, f32[4096]{0:T(1024)}, u32[]{:S(2)}) copy-start(f32[4096]{0:T(1024)} %param.12) | copy-start | bytes 49156
  3.3 11.3 %all-to-all-start = ((bf16[8,16,128]{2,1,0:T(8,128)(2,1)}), bf16[8,16,128]{2,1,0:T(8,128)(2,1)S(1)}, u32[]{:S(2)}, u32[]{:S(2)}) async-start(bf16[8,16,128]{2,1,0:T(8,128)(2,1)} %pick.1), calls=%async_computation | async-start | bytes 65536 | tf_op jit(solution)/shard_map/all_to_all | solution.py:36
  15.3 19.7 %all-to-all-start.1 = ((bf16[32,16,128]{2,1,0:T(8,128)(2,1)}), bf16[32,16,128]{2,1,0:T(8,128)(2,1)S(1)}, u32[]{:S(2)}, u32[]{:S(2)}) async-start(bf16[32,16,128]{2,1,0:T(8,128)(2,1)} %broadcast_in_dim.2), calls=%async_computation.1 | async-start | bytes 262144 | tf_op jit(solution)/shard_map/all_to_all | solution.py:36
  35.0 13.4 %copy-start.1 = (bf16[128,4096]{1,0:T(8,128)(2,1)S(1)}, bf16[128,4096]{1,0:T(8,128)(2,1)}, u32[]{:S(2)}) copy-start(bf16[128,4096]{1,0:T(8,128)(2,1)} %w_out.1) | copy-start | bytes 3145732
  49.4 13.0 %all-to-all-start.3 = ((bf16[32,16,128]{2,1,0:T(8,128)(2,1)}), bf16[32,16,128]{2,1,0:T(8,128)(2,1)S(1)}, u32[]{:S(2)}, u32[]{:S(2)}) async-start(bf16[32,16,128]{2,1,0:T(8,128)(2,1)} %merge.1.after), calls=%async_computation.3 | async-start | bytes 262144 | tf_op jit(solution)/shard_map/all_to_all | solution.py:36
  82.9 23.6 %all-to-all-start.5 = ((f32[256,1,128]{2,1,0:T(1,128)}), f32[256,1,128]{2,1,0:T(1,128)S(1)}, u32[]{:S(2)}, u32[]{:S(2)}) async-start(f32[256,1,128]{2,1,0:T(1,128)} %get-tuple-element.14), calls=%async_computation.5 | async-start | bytes 262144 | tf_op jit(solution)/shard_map/all_to_all | solution.py:36

commit v4 on v3

--- a/solution.py
+++ b/solution.py
@@ -24,10 +24,10 @@
 MIB = 1024 * 1024
 PICK_GRANT = 61 * MIB
 STAGE_GRANT = 49 * MIB + MIB // 2
-ATTEND_GRANT = 206 * MIB // 4
-HEAD_GRANT = 202 * MIB // 4
-W_STAGED = 16
-STAGED = 22
+ATTEND_GRANT = 203 * MIB // 4
+HEAD_GRANT = 201 * MIB // 4
+W_STAGED = 22
+STAGED = 23
 SMEM = pl.BlockSpec(memory_space=pltpu.SMEM)
 HBM = pl.BlockSpec(memory_space=pltpu.HBM)
 
@@ -66,9 +66,10 @@
         copy.start()
         copies.append(copy)
         within.append(jnp.where(inside, offset, TILE))
+    for copy in copies:
+        copy.wait()
     total = jnp.zeros((TILE, HD), f32)
-    for row, copy in enumerate(copies):
-        copy.wait()
+    for row in range(2 * streams):
         block = groups[row].astype(f32)
         found = jnp.sum(jnp.where(row_of() == within[row], block, 0.0), 0, keepdims=True)
         total = jnp.where(row_of() == row, found, total)
@@ -274,12 +275,12 @@
 
 def finish_kernel(shares, lines, out):
     every = lines[...]
-    highest = jnp.max(every, 0, keepdims=True)
-    scaled = pltpu.roll(every, HD // 2, 2) * jnp.exp(every - highest)
-    summed = jnp.sum(scaled, 0)
+    highest = jnp.max(jnp.max(every, 0), 0, keepdims=True)
+    scaled = jnp.exp(every - highest.reshape(1, 1, HD)) * pltpu.roll(every, HD // 2, 2)
+    summed = jnp.sum(jnp.sum(scaled, 0), 0, keepdims=True)
     lane = lax.broadcasted_iota(jnp.int32, summed.shape, 1)
     summed = jnp.where(lane < TILE, summed, 1.0)
-    total = as_column(highest[0] + jnp.log(summed))
+    total = as_column(highest + jnp.log(summed))
     logprobs = shares[...] - total
     streams = out.shape[0]
     for b in range(streams):
@@ -392,7 +393,7 @@
     everyone = seqs * peers
     shares, lines = pl.pallas_call(
         functools.partial(share_kernel, model_width),
-        out_shape=(shape((TILE, share_width), f32), shape((everyone, 1, HD), f32)),
+        out_shape=(shape((TILE, share_width), f32), shape((everyone // 8, 8, HD), f32)),
         in_specs=[VMEM],
         out_specs=(VMEM, VMEM),
         compiler_params=params,
@@ -405,7 +406,7 @@
         out_specs=VMEM,
         compiler_params=params,
         name="finish",
-    )(shares, exchange(lines, EVERYONE))
+    )(shares, exchange(lines.reshape(everyone, 1, HD), EVERYONE).reshape(lines.shape))
     return (
         hidden[:rows].reshape(2, streams, local_width),
         new_kv[:, :rows].reshape(2, 2, streams, local_width),

time: 108 us -> 108 us (level)
  no operation moved by 1% of the time
where the time goes in v4:
time: 108 us; the launch traced here: 107 us
  starting transfers between devices  31.5 us (29%)
  waiting for transfers between devices  31 us (29%)
  blocking collectives  27 us (25%)
  Pallas kernels  14.4 us (13%)
  local copies, waits for them, and re-layouts  2.05 us (2%)
    all_to_all x4, starting transfers between devices, exchange(): return lax.all_to_all(copies, axis, split_axis=0, concat_axis=0, tiled=True)  31.5 us
    all_to_all x4, waiting for transfers between devices, exchange(): return lax.all_to_all(copies, axis, split_axis=0, concat_axis=0, tiled=True)  31 us
    all_to_all x2, blocking collectives, exchange(): return lax.all_to_all(copies, axis, split_axis=0, concat_axis=0, tiled=True)  27 us
    pallas_call x1, Pallas kernels, body(): pl.pallas_call(attend_kernel, out_shape=(shape((seqs, TILE, HD), f32), sh...  3.87 us
    pallas_call x2, Pallas kernels, staged(): pl.pallas_call(stage_kernel, out_shape=jax.ShapeDtypeStruct(shape, source...  3.4 us
    pallas_call x1, Pallas kernels, body(): pl.pallas_call(pick_kernel, out_shape=shape((seqs, TILE, HD), bf16), in_s...  2.59 us
  transfers between devices with their start and end apart: 4, of which 4 were waited for; matrix products, arithmetic and copies ran while one was open for 1% of the time, Pallas kernels for 3%

profile of v4, /device:TPU:1, one launch (start us, length us, event | category | flops | bytes accessed | tf_op | source)
XLA Modules:
  0.0 107.0 jit_solution(16792387794372147510)
XLA Ops:
  0.6 0.0 copy-start
  0.6 0.0 copy-start.3
  0.7 2.6 %pick.1 = bf16[8,16,128]{2,1,0:T(8,128)(2,1)} custom-call(s32[1]{0:T(128)} %bitcast.place, s32[2,7]{1,0:T(2,128)} %ids.1, bf16[16384,128]{1,0:T(8,128)(2,1)} %whole_table.1), custom_call_target="tpu_custom_call" | custom-call | bytes 131072 | tf_op jit(solution)/shard_map/pick/pallas_call | solution.py:312
  3.3 0.0 copy-start.2
  3.3 6.6 %all-to-all-start = ((bf16[8,16,128]{2,1,0:T(8,128)(2,1)}), bf16[8,16,128]{2,1,0:T(8,128)(2,1)S(1)}, u32[]{:S(2)}, u32[]{:S(2)}) async-start(bf16[8,16,128]{2,1,0:T(8,128)(2,1)} %pick.1), calls=%async_computation | async-start | bytes 65536 | tf_op jit(solution)/shard_map/all_to_all | solution.py:36
  9.9 0.0 copy-done.3
  9.9 0.1 convert_element_type.16
  10.0 4.6 %all-to-all-done = bf16[8,16,128]{2,1,0:T(8,128)(2,1)S(1)} async-done(((bf16[8,16,128]{2,1,0:T(8,128)(2,1)}), bf16[8,16,128]{2,1,0:T(8,128)(2,1)S(1)}, u32[]{:S(2)}, u32[]{:S(2)}) %all-to-all-start) | async-done | bytes 32800 | tf_op jit(solution)/shard_map/all_to_all | solution.py:36
  14.6 0.7 broadcast_in_dim.2
  15.3 10.5 %all-to-all-start.1 = ((bf16[32,16,128]{2,1,0:T(8,128)(2,1)}), bf16[32,16,128]{2,1,0:T(8,128)(2,1)S(1)}, u32[]{:S(2)}, u32[]{:S(2)}) async-start(bf16[32,16,128]{2,1,0:T(8,128)(2,1)} %broadcast_in_dim.2), calls=%async_computation.1 | async-start | bytes 262144 | tf_op jit(solution)/shard_map/all_to_all | solution.py:36
  25.8 0.1 fusion
  25.9 0.1 select_maximum_fusion
  26.0 1.6 %stage.2.w_start = bf16[3,2816,128]{2,1,0:T(8,128)(2,1)S(1)} custom-call(bf16[16,128]{1,0:T(8,128)(2,1)S(1)} %reduce_sum.12.after.embedded, bf16[3,4096,128]{2,1,0:T(8,128)(2,1)} %bitcast.17), custom_call_target="tpu_custom_call" | custom-call | bytes 4325376 | tf_op jit(solution)/shard_map/stage/pallas_call | solution.py:97
  27.6 7.4 %all-to-all-done.1.gathered = bf16[32,16,128]{2,1,0:T(8,128)(2,1)S(1)} async-done(((bf16[32,16,128]{2,1,0:T(8,128)(2,1)}), bf16[32,16,128]{2,1,0:T(8,128)(2,1)S(1)}, u32[]{:S(2)}, u32[]{:S(2)}) %all-to-all-start.1) | async-done | bytes 131104 | tf_op jit(solution)/shard_map/all_to_all | solution.py:36
  34.9 0.0 copy-done.2
  34.9 0.0 copy-start.1
  34.9 3.9 %attend.1 = (f32[8,16,128]{2,1,0:T(8,128)S(1)}, bf16[2,16,128]{2,1,0:T(8,128)(2,1)S(1)}) custom-call(s32[1]{0:T(128)} %bitcast.place, s32[7]{0:T(128)S(1)} %copy-done.3, bf16[32,16,128]{2,1,0:T(8,128)(2,1)S(1)} %all-to-all-done.1.gathered, f32[32,128]{1,0:T(8,128)S(1)} %bitcast.14, f32[16,128]{1,0:T(8,128)S(1)} %get-tuple-element.28.cosine, ...), custom_call_target="tpu_custom_call" | custom-call | tf_op jit(solution)/shard_map/attend/pallas_call | solution.py:339
  38.8 9.4 %all_to_all.30.parts = f32[8,16,128]{2,1,0:T(8,128)S(1)} all-to-all(f32[8,16,128]{2,1,0:T(8,128)S(1)} %get-tuple-element.9), channel_id=1, replica_groups=mesh['seq_0'=4,'seq_1'=2,'tensor_0'=4,'tensor_1'=8] {'seq_0','seq_1'}, dimensions={0} | all-to-all | bytes 131072 | tf_op jit(solution)/shard_map/all_to_all | solution.py:36
  48.2 0.0 copy-done.1
  48.2 1.0 merge.1.after
  49.2 3.9 %all-to-all-start.3 = ((bf16[32,16,128]{2,1,0:T(8,128)(2,1)}), bf16[32,16,128]{2,1,0:T(8,128)(2,1)S(1)}, u32[]{:S(2)}, u32[]{:S(2)}) async-start(bf16[32,16,128]{2,1,0:T(8,128)(2,1)} %merge.1.after), calls=%async_computation.3 | async-start | bytes 262144 | tf_op jit(solution)/shard_map/all_to_all | solution.py:36
  53.0 0.0 copy-done
  53.0 0.1 dynamic-slice_bitcast_fusion.gain
  53.1 1.8 %stage.3.staged = bf16[11776,128]{1,0:T(8,128)(2,1)S(1)} custom-call(bf16[32,16,128]{2,1,0:T(8,128)(2,1)} %merge.1.after, bf16[16384,128]{1,0:T(8,128)(2,1)} %whole_table.1), custom_call_target="tpu_custom_call" | custom-call | bytes 6029312 | tf_op jit(solution)/shard_map/stage/pallas_call | solution.py:97
  55.0 7.2 %all-to-all-done.3.parts = bf16[32,16,128]{2,1,0:T(8,128)(2,1)S(1)} async-done(((bf16[32,16,128]{2,1,0:T(8,128)(2,1)}), bf16[32,16,128]{2,1,0:T(8,128)(2,1)S(1)}, u32[]{:S(2)}, u32[]{:S(2)}) %all-to-all-start.3) | async-done | bytes 131104 | tf_op jit(solution)/shard_map/all_to_all | solution.py:36
  62.2 1.7 %head.1 = (bf16[16,128]{1,0:T(8,128)(2,1)S(1)}, bf16[32,16,512]{2,1,0:T(8,128)(2,1)S(1)}) custom-call(bf16[32,16,128]{2,1,0:T(8,128)(2,1)S(1)} %all-to-all-done.3.parts, bf16[16,128]{1,0:T(8,128)(2,1)S(1)} %reduce_sum.12.after.embedded, f32[1,128]{1,0:T(1,128)S(1)} %dynamic-slice_bitcast_fusion.gain, bf16[11776,128]{1,0:T(8,128)(2,1)S(1)} %stage.3.staged, ...), custom_call_target="tpu_custom_call" | custom-call | tf_op jit(solution)/shard_map/head/pallas_call | solution.py:375
  63.9 17.6 %all_to_all.31.parts = bf16[32,16,512]{2,1,0:T(8,128)(2,1)S(1)} all-to-all(bf16[32,16,512]{2,1,0:T(8,128)(2,1)S(1)} %get-tuple-element.12), channel_id=1, replica_groups=mesh['seq_0'=4,'seq_1'=2,'tensor_0'=4,'tensor_1'=8] {'tensor_0','tensor_1'}, dimensions={0} | all-to-all | bytes 1048576 | tf_op jit(solution)/shard_map/all_to_all | solution.py:36
  81.6 1.0 share.1
  82.6 10.6 %all-to-all-start.5 = ((f32[256,1,128]{2,1,0:T(1,128)}), f32[256,1,128]{2,1,0:T(1,128)S(1)}, u32[]{:S(2)}, u32[]{:S(2)}) async-start(f32[256,1,128]{2,1,0:T(1,128)} %bitcast.6), calls=%async_computation.5 | async-start | bytes 262144 | tf_op jit(solution)/shard_map/all_to_all | solution.py:36
  93.2 0.6 copy.20
  93.8 0.6 copy.19
  94.4 11.8 %all-to-all-done.5 = f32[256,1,128]{2,1,0:T(1,128)S(1)} async-done(((f32[256,1,128]{2,1,0:T(1,128)}), f32[256,1,128]{2,1,0:T(1,128)S(1)}, u32[]{:S(2)}, u32[]{:S(2)}) %all-to-all-start.5) | async-done | bytes 131104 | tf_op jit(solution)/shard_map/all_to_all | solution.py:36
  106.2 0.8 finish.1
  (5 shorter events, 0.0 us)
Async XLA Ops:
  0.6 52.4 %copy-start = (f32[4096]{0:T(1024)S(1)}, f32[4096]{0:T(1024)}, u32[]{:S(2)}) copy-start(f32[4096]{0:T(1024)} %param.13) | copy-start | bytes 49156
  0.6 9.2 %copy-start.3 = (s32[7]{0:T(128)S(1)}, s32[7]{0:T(128)}, u32[]{:S(2)}) copy-start(s32[7]{0:T(128)} %lengths.1) | copy-start | bytes 88
  3.3 31.7 %copy-start.2 = (f32[4096]{0:T(1024)S(1)}, f32[4096]{0:T(1024)}, u32[]{:S(2)}) copy-start(f32[4096]{0:T(1024)} %param.12) | copy-start | bytes 49156
  3.3 11.3 %all-to-all-start = ((bf16[8,16,128]{2,1,0:T(8,128)(2,1)}), bf16[8,16,128]{2,1,0:T(8,128)(2,1)S(1)}, u32[]{:S(2)}, u32[]{:S(2)}) async-start(bf16[8,16,128]{2,1,0:T(8,128)(2,1)} %pick.1), calls=%async_computation | async-start | bytes 65536 | tf_op jit(solution)/shard_map/all_to_all | solution.py:36
  15.3 19.6 %all-to-all-start.1 = ((bf16[32,16,128]{2,1,0:T(8,128)(2,1)}), bf16[32,16,128]{2,1,0:T(8,128)(2,1)S(1)}, u32[]{:S(2)}, u32[]{:S(2)}) async-start(bf16[32,16,128]{2,1,0:T(8,128)(2,1)} %broadcast_in_dim.2), calls=%async_computation.1 | async-start | bytes 262144 | tf_op jit(solution)/shard_map/all_to_all | solution.py:36
  34.9 13.2 %copy-start.1 = (bf16[128,4096]{1,0:T(8,128)(2,1)S(1)}, bf16[128,4096]{1,0:T(8,128)(2,1)}, u32[]{:S(2)}) copy-start(bf16[128,4096]{1,0:T(8,128)(2,1)} %w_out.1) | copy-start | bytes 3145732
  49.2 13.0 %all-to-all-start.3 = ((bf16[32,16,128]{2,1,0:T(8,128)(2,1)}), bf16[32,16,128]{2,1,0:T(8,128)(2,1)S(1)}, u32[]{:S(2)}, u32[]{:S(2)}) async-start(bf16[32,16,128]{2,1,0:T(8,128)(2,1)} %merge.1.after), calls=%async_computation.3 | async-start | bytes 262144 | tf_op jit(solution)/shard_map/all_to_all | solution.py:36
  82.6 23.6 %all-to-all-start.5 = ((f32[256,1,128]{2,1,0:T(1,128)}), f32[256,1,128]{2,1,0:T(1,128)S(1)}, u32[]{:S(2)}, u32[]{:S(2)}) async-start(f32[256,1,128]{2,1,0:T(1,128)} %bitcast.6), calls=%async_computation.5 | async-start | bytes 262144 | tf_op jit(solution)/shard_map/all_to_all | solution.py:36

commit v5 on v4

--- a/solution.py
+++ b/solution.py
@@ -52,6 +52,22 @@
     return jnp.sum(jnp.where(row_of() == lane_of(), line, 0.0), 1, keepdims=True)
 
 
+def thirds(value):
+    high = value.astype(bf16).astype(f32)
+    middle = (value - high).astype(bf16).astype(f32)
+    return high, middle, value - high - middle
+
+
+def packed(column):
+    high, middle, low = thirds(as_line(column))
+    return high + pltpu.roll(middle, TILE, 1) + pltpu.roll(low, 2 * TILE, 1)
+
+
+def unpacked(line):
+    line = line + pltpu.roll(line, HD - TILE, 1) + pltpu.roll(line, HD - 2 * TILE, 1)
+    return as_column(line)
+
+
 def pick_kernel(place, ids, table, out, groups, sems):
     streams = ids.shape[1]
     vocab_rows = table.shape[0]
@@ -60,19 +76,22 @@
         local = ids[row // streams, row % streams] - place[0] * vocab_rows
         inside = (local >= 0) & (local < vocab_rows)
         local = jnp.clip(local, 0, vocab_rows - 1)
-        offset = lax.rem(local, TILE)
+        offset = local & (TILE - 1)
         start = pl.multiple_of(local - offset, TILE)
-        copy = pltpu.make_async_copy(table.at[pl.ds(start, TILE)], groups.at[row], sems.at[row])
+        copy = pltpu.make_async_copy(
+            table.at[pl.ds(start, TILE)], groups.at[pl.ds(row * TILE, TILE)], sems.at[row]
+        )
         copy.start()
         copies.append(copy)
-        within.append(jnp.where(inside, offset, TILE))
+        within.append(jnp.where(inside, row * TILE + offset, -1))
     for copy in copies:
         copy.wait()
-    total = jnp.zeros((TILE, HD), f32)
-    for row in range(2 * streams):
-        block = groups[row].astype(f32)
-        found = jnp.sum(jnp.where(row_of() == within[row], block, 0.0), 0, keepdims=True)
-        total = jnp.where(row_of() == row, found, total)
+    row_at = row_of(groups.shape[0])
+    target = jnp.full(row_at.shape, -1, jnp.int32)
+    for row, at in enumerate(within):
+        target = jnp.where(row_at == row, at, target)
+    chosen = (target == lane_of(groups.shape[0])).astype(f32).astype(bf16)
+    total = jnp.dot(chosen, groups[...], preferred_element_type=f32)
     picked = total.astype(bf16)
     for peer in range(out.shape[0]):
         out[peer] = picked
@@ -198,22 +217,22 @@
         mine = (rows == b) | (rows == streams + b)
         share = jnp.where(mine, weights, 0.0).astype(bf16)
         mixed = mixed + jnp.dot(share, values[b], preferred_element_type=f32)
-    sent = jnp.where(row_of() == TILE - 2, as_line(highest), mixed)
-    sent = jnp.where(row_of() == TILE - 1, as_line(total), sent)
+    sent = jnp.where(row_of() == TILE - 2, packed(highest), mixed)
+    sent = jnp.where(row_of() == TILE - 1, packed(total), sent).astype(bf16)
     for peer in range(out.shape[0]):
         out[peer] = sent
 
 
 def merge_kernel(rows, parts, w_out, out):
-    count = parts.shape[0]
-    peaks = [as_column(parts[k, TILE - 2 : TILE - 1, :]) for k in range(count)]
+    blocks = [parts[k].astype(f32) for k in range(parts.shape[0])]
+    peaks = [unpacked(block[TILE - 2 : TILE - 1, :]) for block in blocks]
     highest = functools.reduce(jnp.maximum, peaks)
     numerator = jnp.zeros((TILE, HD), f32)
     denominator = jnp.zeros((TILE, 1), f32)
-    for k in range(count):
-        scale = jnp.exp(peaks[k] - highest)
-        numerator = numerator + parts[k] * scale
-        denominator = denominator + as_column(parts[k, TILE - 1 : TILE, :]) * scale
+    for block, peak in zip(blocks, peaks):
+        scale = jnp.exp(peak - highest)
+        numerator = numerator + block * scale
+        denominator = denominator + unpacked(block[TILE - 1 : TILE, :]) * scale
     real = row_of() < rows
     attended = jnp.where(real, numerator / jnp.where(real, denominator, 1.0), 0.0).astype(bf16)
     per = 8
@@ -239,10 +258,7 @@
     hidden_out[...] = hidden
     wide = hidden.astype(f32)
     squares = as_line(jnp.sum(wide * wide, 1, keepdims=True))
-    high = squares.astype(bf16).astype(f32)
-    middle = (squares - high).astype(bf16).astype(f32)
-    low = squares - high - middle
-    line = jnp.concatenate([high, middle, low, jnp.zeros((1, share - 3 * HD), f32)], 1)
+    line = jnp.concatenate([*thirds(squares), jnp.zeros((1, share - 3 * HD), f32)], 1)
     gated = (wide * gain[...]).astype(bf16)
     spare = row_of(share) == TILE - 1
     for k in range(peers):
@@ -315,7 +331,7 @@
         in_specs=[SMEM, SMEM, HBM],
         out_specs=VMEM,
         scratch_shapes=[
-            pltpu.VMEM((rows, TILE, HD), bf16),
+            pltpu.VMEM((rows * TILE, HD), bf16),
             pltpu.SemaphoreType.DMA((rows,)),
         ],
         compiler_params=pltpu.CompilerParams(vmem_limit_bytes=PICK_GRANT),
@@ -338,7 +354,7 @@
     w_rows = model_width * W_STAGED // 32
     parts, new_kv = pl.pallas_call(
         attend_kernel,
-        out_shape=(shape((seqs, TILE, HD), f32), shape((2, TILE, HD), bf16)),
+        out_shape=(shape((seqs, TILE, HD), bf16), shape((2, TILE, HD), bf16)),
         in_specs=[SMEM, SMEM] + [VMEM] * 5 + [HBM] * 3,
         out_specs=(VMEM, VMEM),
         scratch_shapes=[

time: 108 us -> 108 us (level)
  no operation moved by 1% of the time
where the time goes in v5:
time: 108 us; the launch traced here: 107 us
  starting transfers between devices  31.3 us (29%)
  waiting for transfers between devices  31 us (29%)
  blocking collectives  27 us (25%)
  Pallas kernels  14.7 us (14%)
  local copies, waits for them, and re-layouts  2.05 us (2%)
    all_to_all x4, starting transfers between devices, exchange(): return lax.all_to_all(copies, axis, split_axis=0, concat_axis=0, tiled=True)  31.3 us
    all_to_all x4, waiting for transfers between devices, exchange(): return lax.all_to_all(copies, axis, split_axis=0, concat_axis=0, tiled=True)  31 us
    all_to_all x2, blocking collectives, exchange(): return lax.all_to_all(copies, axis, split_axis=0, concat_axis=0, tiled=True)  27 us
    pallas_call x1, Pallas kernels, body(): pl.pallas_call(attend_kernel, out_shape=(shape((seqs, TILE, HD), bf16), s...  3.87 us
    pallas_call x2, Pallas kernels, staged(): pl.pallas_call(stage_kernel, out_shape=jax.ShapeDtypeStruct(shape, source...  3.4 us
    pallas_call x1, Pallas kernels, body(): pl.pallas_call(pick_kernel, out_shape=shape((seqs, TILE, HD), bf16), in_s...  2.81 us
  transfers between devices with their start and end apart: 4, of which 4 were waited for; matrix products, arithmetic and copies ran while one was open for 1% of the time, Pallas kernels for 3%

profile of v5, /device:TPU:1, one launch (start us, length us, event | category | flops | bytes accessed | tf_op | source)
XLA Modules:
  0.0 107.1 jit_solution(5860032272883843216)
XLA Ops:
  0.6 0.0 copy-start
  0.6 0.0 copy-start.3
  0.7 2.8 %pick.1 = bf16[8,16,128]{2,1,0:T(8,128)(2,1)} custom-call(s32[1]{0:T(128)} %bitcast.place, s32[2,7]{1,0:T(2,128)} %ids.1, bf16[16384,128]{1,0:T(8,128)(2,1)} %whole_table.1), custom_call_target="tpu_custom_call" | custom-call | bytes 131072 | tf_op jit(solution)/shard_map/pick/pallas_call | solution.py:328
  3.5 0.0 copy-start.2
  3.5 6.5 %all-to-all-start = ((bf16[8,16,128]{2,1,0:T(8,128)(2,1)}), bf16[8,16,128]{2,1,0:T(8,128)(2,1)S(1)}, u32[]{:S(2)}, u32[]{:S(2)}) async-start(bf16[8,16,128]{2,1,0:T(8,128)(2,1)} %pick.1), calls=%async_computation | async-start | bytes 65536 | tf_op jit(solution)/shard_map/all_to_all | solution.py:36
  10.0 0.0 copy-done.3
  10.0 0.1 convert_element_type.16
  10.1 4.6 %all-to-all-done = bf16[8,16,128]{2,1,0:T(8,128)(2,1)S(1)} async-done(((bf16[8,16,128]{2,1,0:T(8,128)(2,1)}), bf16[8,16,128]{2,1,0:T(8,128)(2,1)S(1)}, u32[]{:S(2)}, u32[]{:S(2)}) %all-to-all-start) | async-done | bytes 32800 | tf_op jit(solution)/shard_map/all_to_all | solution.py:36
  14.7 0.7 broadcast_in_dim.2
  15.4 10.5 %all-to-all-start.1 = ((bf16[32,16,128]{2,1,0:T(8,128)(2,1)}), bf16[32,16,128]{2,1,0:T(8,128)(2,1)S(1)}, u32[]{:S(2)}, u32[]{:S(2)}) async-start(bf16[32,16,128]{2,1,0:T(8,128)(2,1)} %broadcast_in_dim.2), calls=%async_computation.1 | async-start | bytes 262144 | tf_op jit(solution)/shard_map/all_to_all | solution.py:36
  25.9 0.1 fusion
  26.0 0.1 select_maximum_fusion
  26.1 1.6 %stage.2.w_start = bf16[3,2816,128]{2,1,0:T(8,128)(2,1)S(1)} custom-call(bf16[16,128]{1,0:T(8,128)(2,1)S(1)} %reduce_sum.12.after.embedded, bf16[3,4096,128]{2,1,0:T(8,128)(2,1)} %bitcast.17), custom_call_target="tpu_custom_call" | custom-call | bytes 4325376 | tf_op jit(solution)/shard_map/stage/pallas_call | solution.py:116
  27.7 7.4 %all-to-all-done.1.gathered = bf16[32,16,128]{2,1,0:T(8,128)(2,1)S(1)} async-done(((bf16[32,16,128]{2,1,0:T(8,128)(2,1)}), bf16[32,16,128]{2,1,0:T(8,128)(2,1)S(1)}, u32[]{:S(2)}, u32[]{:S(2)}) %all-to-all-start.1) | async-done | bytes 131104 | tf_op jit(solution)/shard_map/all_to_all | solution.py:36
  35.0 0.0 copy-done.2
  35.0 0.0 copy-start.1
  35.0 3.9 %attend.1 = (bf16[8,16,128]{2,1,0:T(8,128)(2,1)S(1)}, bf16[2,16,128]{2,1,0:T(8,128)(2,1)S(1)}) custom-call(s32[1]{0:T(128)} %bitcast.place, s32[7]{0:T(128)S(1)} %copy-done.3, bf16[32,16,128]{2,1,0:T(8,128)(2,1)S(1)} %all-to-all-done.1.gathered, f32[32,128]{1,0:T(8,128)S(1)} %bitcast.14, f32[16,128]{1,0:T(8,128)S(1)} %get-tuple-element.28.cosine, ...), custom_call_target="tpu_custom_call" | custom-call | tf_op jit(solution)/shard_map/attend/pallas_call | solution.py:355
  38.9 9.2 %all_to_all.30.parts = bf16[8,16,128]{2,1,0:T(8,128)(2,1)S(1)} all-to-all(bf16[8,16,128]{2,1,0:T(8,128)(2,1)S(1)} %get-tuple-element.9), channel_id=1, replica_groups=mesh['seq_0'=4,'seq_1'=2,'tensor_0'=4,'tensor_1'=8] {'seq_0','seq_1'}, dimensions={0} | all-to-all | bytes 65536 | tf_op jit(solution)/shard_map/all_to_all | solution.py:36
  48.1 0.0 copy-done.1
  48.1 1.1 %merge.1.after = bf16[32,16,128]{2,1,0:T(8,128)(2,1)} custom-call(bf16[8,16,128]{2,1,0:T(8,128)(2,1)S(1)} %all_to_all.30.parts, bf16[128,4096]{1,0:T(8,128)(2,1)S(1)} %copy-done.1), custom_call_target="tpu_custom_call" | custom-call | tf_op jit(solution)/shard_map/merge/pallas_call | solution.py:380
  49.2 3.9 %all-to-all-start.3 = ((bf16[32,16,128]{2,1,0:T(8,128)(2,1)}), bf16[32,16,128]{2,1,0:T(8,128)(2,1)S(1)}, u32[]{:S(2)}, u32[]{:S(2)}) async-start(bf16[32,16,128]{2,1,0:T(8,128)(2,1)} %merge.1.after), calls=%async_computation.3 | async-start | bytes 262144 | tf_op jit(solution)/shard_map/all_to_all | solution.py:36
  53.1 0.0 copy-done
  53.1 0.1 dynamic-slice_bitcast_fusion.gain
  53.2 1.8 %stage.3.staged = bf16[11776,128]{1,0:T(8,128)(2,1)S(1)} custom-call(bf16[32,16,128]{2,1,0:T(8,128)(2,1)} %merge.1.after, bf16[16384,128]{1,0:T(8,128)(2,1)} %whole_table.1), custom_call_target="tpu_custom_call" | custom-call | bytes 6029312 | tf_op jit(solution)/shard_map/stage/pallas_call | solution.py:116
  55.0 7.2 %all-to-all-done.3.parts = bf16[32,16,128]{2,1,0:T(8,128)(2,1)S(1)} async-done(((bf16[32,16,128]{2,1,0:T(8,128)(2,1)}), bf16[32,16,128]{2,1,0:T(8,128)(2,1)S(1)}, u32[]{:S(2)}, u32[]{:S(2)}) %all-to-all-start.3) | async-done | bytes 131104 | tf_op jit(solution)/shard_map/all_to_all | solution.py:36
  62.2 1.7 %head.1 = (bf16[16,128]{1,0:T(8,128)(2,1)S(1)}, bf16[32,16,512]{2,1,0:T(8,128)(2,1)S(1)}) custom-call(bf16[32,16,128]{2,1,0:T(8,128)(2,1)S(1)} %all-to-all-done.3.parts, bf16[16,128]{1,0:T(8,128)(2,1)S(1)} %reduce_sum.12.after.embedded, f32[1,128]{1,0:T(1,128)S(1)} %dynamic-slice_bitcast_fusion.gain, bf16[11776,128]{1,0:T(8,128)(2,1)S(1)} %stage.3.staged, ...), custom_call_target="tpu_custom_call" | custom-call | tf_op jit(solution)/shard_map/head/pallas_call | solution.py:391
  64.0 17.8 %all_to_all.31.parts = bf16[32,16,512]{2,1,0:T(8,128)(2,1)S(1)} all-to-all(bf16[32,16,512]{2,1,0:T(8,128)(2,1)S(1)} %get-tuple-element.12), channel_id=1, replica_groups=mesh['seq_0'=4,'seq_1'=2,'tensor_0'=4,'tensor_1'=8] {'tensor_0','tensor_1'}, dimensions={0} | all-to-all | bytes 1048576 | tf_op jit(solution)/shard_map/all_to_all | solution.py:36
  81.8 1.0 share.1
  82.8 10.5 %all-to-all-start.5 = ((f32[256,1,128]{2,1,0:T(1,128)}), f32[256,1,128]{2,1,0:T(1,128)S(1)}, u32[]{:S(2)}, u32[]{:S(2)}) async-start(f32[256,1,128]{2,1,0:T(1,128)} %bitcast.6), calls=%async_computation.5 | async-start | bytes 262144 | tf_op jit(solution)/shard_map/all_to_all | solution.py:36
  93.3 0.6 copy.20
  94.0 0.6 copy.19
  94.5 11.8 %all-to-all-done.5 = f32[256,1,128]{2,1,0:T(1,128)S(1)} async-done(((f32[256,1,128]{2,1,0:T(1,128)}), f32[256,1,128]{2,1,0:T(1,128)S(1)}, u32[]{:S(2)}, u32[]{:S(2)}) %all-to-all-start.5) | async-done | bytes 131104 | tf_op jit(solution)/shard_map/all_to_all | solution.py:36
  106.3 0.8 finish.1
  (5 shorter events, 0.0 us)
Async XLA Ops:
  0.6 52.5 %copy-start = (f32[4096]{0:T(1024)S(1)}, f32[4096]{0:T(1024)}, u32[]{:S(2)}) copy-start(f32[4096]{0:T(1024)} %param.13) | copy-start | bytes 49156
  0.6 9.3 %copy-start.3 = (s32[7]{0:T(128)S(1)}, s32[7]{0:T(128)}, u32[]{:S(2)}) copy-start(s32[7]{0:T(128)} %lengths.1) | copy-start | bytes 88
  3.5 31.6 %copy-start.2 = (f32[4096]{0:T(1024)S(1)}, f32[4096]{0:T(1024)}, u32[]{:S(2)}) copy-start(f32[4096]{0:T(1024)} %param.12) | copy-start | bytes 49156
  3.5 11.2 %all-to-all-start = ((bf16[8,16,128]{2,1,0:T(8,128)(2,1)}), bf16[8,16,128]{2,1,0:T(8,128)(2,1)S(1)}, u32[]{:S(2)}, u32[]{:S(2)}) async-start(bf16[8,16,128]{2,1,0:T(8,128)(2,1)} %pick.1), calls=%async_computation | async-start | bytes 65536 | tf_op jit(solution)/shard_map/all_to_all | solution.py:36
  15.4 19.7 %all-to-all-start.1 = ((bf16[32,16,128]{2,1,0:T(8,128)(2,1)}), bf16[32,16,128]{2,1,0:T(8,128)(2,1)S(1)}, u32[]{:S(2)}, u32[]{:S(2)}) async-start(bf16[32,16,128]{2,1,0:T(8,128)(2,1)} %broadcast_in_dim.2), calls=%async_computation.1 | async-start | bytes 262144 | tf_op jit(solution)/shard_map/all_to_all | solution.py:36
  35.0 13.1 %copy-start.1 = (bf16[128,4096]{1,0:T(8,128)(2,1)S(1)}, bf16[128,4096]{1,0:T(8,128)(2,1)}, u32[]{:S(2)}) copy-start(bf16[128,4096]{1,0:T(8,128)(2,1)} %w_out.1) | copy-start | bytes 3145732
  49.2 13.0 %all-to-all-start.3 = ((bf16[32,16,128]{2,1,0:T(8,128)(2,1)}), bf16[32,16,128]{2,1,0:T(8,128)(2,1)S(1)}, u32[]{:S(2)}, u32[]{:S(2)}) async-start(bf16[32,16,128]{2,1,0:T(8,128)(2,1)} %merge.1.after), calls=%async_computation.3 | async-start | bytes 262144 | tf_op jit(solution)/shard_map/all_to_all | solution.py:36
  82.8 23.5 %all-to-all-start.5 = ((f32[256,1,128]{2,1,0:T(1,128)}), f32[256,1,128]{2,1,0:T(1,128)S(1)}, u32[]{:S(2)}, u32[]{:S(2)}) async-start(f32[256,1,128]{2,1,0:T(1,128)} %bitcast.6), calls=%async_computation.5 | async-start | bytes 262144 | tf_op jit(solution)/shard_map/all_to_all | solution.py:36

commit v6 on v4

--- a/solution.py
+++ b/solution.py
@@ -30,6 +30,11 @@
 STAGED = 23
 SMEM = pl.BlockSpec(memory_space=pltpu.SMEM)
 HBM = pl.BlockSpec(memory_space=pltpu.HBM)
+
+
+def slot_of(block):
+    planes, depth = lax.axis_size(TENSOR[0]), lax.axis_size(TENSOR[1])
+    return block % depth * planes + block // depth
 
 
 def exchange(copies, axis):
@@ -109,6 +114,7 @@
 
 
 def attend_kernel(
+    slots_at,
     place,
     lengths,
     gathered,
@@ -144,7 +150,7 @@
         squares = squares + part * part
     scale = lax.rsqrt(jnp.sum(squares, 1, keepdims=True) / width + epsilon)
     normed = [
-        (gathered[k].astype(f32) * scale * gain[k : k + 1]).astype(bf16) for k in range(blocks)
+        (gathered[slots_at[k]].astype(f32) * scale * gain[k : k + 1]).astype(bf16) for k in range(blocks)
     ]
     begin = jnp.concatenate(normed[: first // HD], 1)
     rest = jnp.concatenate(normed[first // HD :], 1)
@@ -204,7 +210,7 @@
         out[peer] = sent
 
 
-def merge_kernel(rows, parts, w_out, out):
+def merge_kernel(rows, slots_at, parts, w_out, out):
     count = parts.shape[0]
     peaks = [as_column(parts[k, TILE - 2 : TILE - 1, :]) for k in range(count)]
     highest = functools.reduce(jnp.maximum, peaks)
@@ -222,10 +228,10 @@
             attended, w_out[:, group * per * HD : (group + 1) * per * HD], preferred_element_type=f32
         ).astype(bf16)
         for k in range(per):
-            out[group * per + k] = some[:, k * HD : (k + 1) * HD]
-
-
-def head_kernel(parts, embedded, gain, staged, whole_table, hidden_out, out, table, sem):
+            out[slots_at[group * per + k]] = some[:, k * HD : (k + 1) * HD]
+
+
+def head_kernel(slots_at, parts, embedded, gain, staged, whole_table, hidden_out, out, table, sem):
     peers, _, share = out.shape
     first = staged.shape[0] // share
     rest = pltpu.make_async_copy(
@@ -255,7 +261,7 @@
             (((1,), (1,)), ((), ())),
             preferred_element_type=f32,
         )
-        out[k] = jnp.where(spare, line, some).astype(bf16)
+        out[slots_at[k]] = jnp.where(spare, line, some).astype(bf16)
 
 
 def share_kernel(model_width, parts, shares_out, lines_out):
@@ -305,6 +311,7 @@
     model_width = attn_gain.shape[0]
     seqs, peers = lax.axis_size(SEQ), lax.axis_size(TENSOR)
     tensor_index = lax.axis_index(TENSOR)
+    slots_at = [slot_of(block) for block in range(peers)]
     place = lax.axis_index(SEQ).astype(jnp.int32).reshape(1)
     params = pltpu.CompilerParams(vmem_limit_bytes=16 * 1024 * 1024)
     shape = jax.ShapeDtypeStruct
@@ -323,7 +330,7 @@
         name="pick",
     )(place, token_ids, embed_table)
     embedded = jnp.sum(exchange(picked, SEQ).astype(f32), 0).astype(bf16)
-    gathered = exchange(jnp.broadcast_to(embedded, (peers, TILE, HD)), TENSOR)
+    gathered = exchange(jnp.broadcast_to(embedded, (peers, TILE, HD)), TENSOR[::-1])
 
     positions = (cache_lengths[None, :] + jnp.arange(2, dtype=jnp.int32)[:, None]).reshape(rows)
     half = HD // 2
@@ -337,7 +344,7 @@
     w_qkv = jnp.moveaxis(w_qkv, 1, 0)
     w_rows = model_width * W_STAGED // 32
     parts, new_kv = pl.pallas_call(
-        attend_kernel,
+        functools.partial(attend_kernel, slots_at),
         out_shape=(shape((seqs, TILE, HD), f32), shape((2, TILE, HD), bf16)),
         in_specs=[SMEM, SMEM] + [VMEM] * 5 + [HBM] * 3,
         out_specs=(VMEM, VMEM),
@@ -362,7 +369,7 @@
         cache_values,
     )
     mixed = pl.pallas_call(
-        functools.partial(merge_kernel, rows),
+        functools.partial(merge_kernel, rows, slots_at),
         out_shape=shape((peers, TILE, HD), bf16),
         in_specs=[VMEM, VMEM],
         out_specs=VMEM,
@@ -373,7 +380,7 @@
     staged_rows = STAGED * peers // 32 * share_width
     table_start = staged(mixed, embed_table, staged_rows)
     hidden, sent = pl.pallas_call(
-        head_kernel,
+        functools.partial(head_kernel, slots_at),
         out_shape=(shape((TILE, HD), bf16), shape((peers, TILE, share_width), bf16)),
         in_specs=[VMEM] * 4 + [HBM],
         out_specs=(VMEM, VMEM),
@@ -384,7 +391,7 @@
         compiler_params=pltpu.CompilerParams(vmem_limit_bytes=HEAD_GRANT),
         name="head",
     )(
-        exchange(mixed, TENSOR),
+        exchange(mixed, TENSOR[::-1]),
         embedded,
         lax.dynamic_slice_in_dim(final_gain, tensor_index * HD, HD).reshape(1, HD),
         table_start,
@@ -398,7 +405,7 @@
         out_specs=(VMEM, VMEM),
         compiler_params=params,
         name="share",
-    )(exchange(sent, TENSOR))
+    )(exchange(sent, TENSOR[::-1]))
     logprobs = pl.pallas_call(
         finish_kernel,
         out_shape=shape((streams, 2, share_width), f32),

time: 108 us -> 107 us (level)
  starting transfers between devices: 31.5 us -> 30 us
    all_to_all x4, starting transfers between devices: 31.5 us -> 30 us  [exchange(): return lax.all_to_all(copies, axis, split_axis=0, concat_axis=0, tiled=True)]
where the time goes in v6:
time: 107 us
  waiting for transfers between devices  31.4 us (29%)
  starting transfers between devices  30 us (28%)
  blocking collectives  27.6 us (26%)
  Pallas kernels  14.6 us (14%)
  local copies, waits for them, and re-layouts  2.05 us (2%)
    all_to_all x4, waiting for transfers between devices, exchange(): return lax.all_to_all(copies, axis, split_axis=0, concat_axis=0, tiled=True)  31.4 us
    all_to_all x4, starting transfers between devices, exchange(): return lax.all_to_all(copies, axis, split_axis=0, concat_axis=0, tiled=True)  30 us
    all_to_all x2, blocking collectives, exchange(): return lax.all_to_all(copies, axis, split_axis=0, concat_axis=0, tiled=True)  27.6 us
    pallas_call x1, Pallas kernels, body(): pl.pallas_call(functools.partial(attend_kernel, slots_at), out_shape=(sha...  3.87 us
    pallas_call x2, Pallas kernels, staged(): pl.pallas_call(stage_kernel, out_shape=jax.ShapeDtypeStruct(shape, source...  3.4 us
    pallas_call x1, Pallas kernels, body(): pl.pallas_call(pick_kernel, out_shape=shape((seqs, TILE, HD), bf16), in_s...  2.74 us
  transfers between devices with their start and end apart: 4, of which 4 were waited for; matrix products, arithmetic and copies ran while one was open for 1% of the time, Pallas kernels for 3%

profile of v6, /device:TPU:1, one launch (start us, length us, event | category | flops | bytes accessed | tf_op | source)
XLA Modules:
  0.0 106.7 jit_solution(1683134391309876423)
XLA Ops:
  0.6 0.0 copy-start
  0.6 0.0 copy-start.3
  0.7 2.7 %pick.1 = bf16[8,16,128]{2,1,0:T(8,128)(2,1)} custom-call(s32[1]{0:T(128)} %bitcast.place, s32[2,7]{1,0:T(2,128)} %ids.1, bf16[16384,128]{1,0:T(8,128)(2,1)} %whole_table.1), custom_call_target="tpu_custom_call" | custom-call | bytes 131072 | tf_op jit(solution)/shard_map/pick/pallas_call | solution.py:319
  3.4 0.0 copy-start.2
  3.4 6.5 %all-to-all-start = ((bf16[8,16,128]{2,1,0:T(8,128)(2,1)}), bf16[8,16,128]{2,1,0:T(8,128)(2,1)S(1)}, u32[]{:S(2)}, u32[]{:S(2)}) async-start(bf16[8,16,128]{2,1,0:T(8,128)(2,1)} %pick.1), calls=%async_computation | async-start | bytes 65536 | tf_op jit(solution)/shard_map/all_to_all | solution.py:41
  9.9 0.0 copy-done.3
  9.9 0.1 convert_element_type.16
  10.0 4.6 %all-to-all-done = bf16[8,16,128]{2,1,0:T(8,128)(2,1)S(1)} async-done(((bf16[8,16,128]{2,1,0:T(8,128)(2,1)}), bf16[8,16,128]{2,1,0:T(8,128)(2,1)S(1)}, u32[]{:S(2)}, u32[]{:S(2)}) %all-to-all-start) | async-done | bytes 32800 | tf_op jit(solution)/shard_map/all_to_all | solution.py:41
  14.6 0.7 broadcast_in_dim.2
  15.3 10.5 %all-to-all-start.1 = ((bf16[32,16,128]{2,1,0:T(8,128)(2,1)}), bf16[32,16,128]{2,1,0:T(8,128)(2,1)S(1)}, u32[]{:S(2)}, u32[]{:S(2)}) async-start(bf16[32,16,128]{2,1,0:T(8,128)(2,1)} %broadcast_in_dim.2), calls=%async_computation.1 | async-start | bytes 262144 | tf_op jit(solution)/shard_map/all_to_all | solution.py:41
  25.8 0.1 fusion
  25.9 0.1 select_maximum_fusion
  26.0 1.6 %stage.2.w_start = bf16[3,2816,128]{2,1,0:T(8,128)(2,1)S(1)} custom-call(bf16[16,128]{1,0:T(8,128)(2,1)S(1)} %reduce_sum.12.after.embedded, bf16[3,4096,128]{2,1,0:T(8,128)(2,1)} %bitcast.17), custom_call_target="tpu_custom_call" | custom-call | bytes 4325376 | tf_op jit(solution)/shard_map/stage/pallas_call | solution.py:102
  27.6 7.6 %all-to-all-done.1.gathered = bf16[32,16,128]{2,1,0:T(8,128)(2,1)S(1)} async-done(((bf16[32,16,128]{2,1,0:T(8,128)(2,1)}), bf16[32,16,128]{2,1,0:T(8,128)(2,1)S(1)}, u32[]{:S(2)}, u32[]{:S(2)}) %all-to-all-start.1) | async-done | bytes 131104 | tf_op jit(solution)/shard_map/all_to_all | solution.py:41
  35.2 0.0 copy-done.2
  35.2 0.0 copy-start.1
  35.2 3.9 %attend.1 = (f32[8,16,128]{2,1,0:T(8,128)S(1)}, bf16[2,16,128]{2,1,0:T(8,128)(2,1)S(1)}) custom-call(s32[1]{0:T(128)} %bitcast.place, s32[7]{0:T(128)S(1)} %copy-done.3, bf16[32,16,128]{2,1,0:T(8,128)(2,1)S(1)} %all-to-all-done.1.gathered, f32[32,128]{1,0:T(8,128)S(1)} %bitcast.14, f32[16,128]{1,0:T(8,128)S(1)} %get-tuple-element.28.cosine, ...), custom_call_target="tpu_custom_call" | custom-call | tf_op jit(solution)/shard_map/attend/pallas_call | solution.py:346
  39.0 9.4 %all_to_all.30.parts = f32[8,16,128]{2,1,0:T(8,128)S(1)} all-to-all(f32[8,16,128]{2,1,0:T(8,128)S(1)} %get-tuple-element.9), channel_id=1, replica_groups=mesh['seq_0'=4,'seq_1'=2,'tensor_0'=4,'tensor_1'=8] {'seq_0','seq_1'}, dimensions={0} | all-to-all | bytes 131072 | tf_op jit(solution)/shard_map/all_to_all | solution.py:41
  48.4 0.0 copy-done.1
  48.4 1.0 merge.1.after
  49.4 3.9 %all-to-all-start.3 = ((bf16[32,16,128]{2,1,0:T(8,128)(2,1)}), bf16[32,16,128]{2,1,0:T(8,128)(2,1)S(1)}, u32[]{:S(2)}, u32[]{:S(2)}) async-start(bf16[32,16,128]{2,1,0:T(8,128)(2,1)} %merge.1.after), calls=%async_computation.3 | async-start | bytes 262144 | tf_op jit(solution)/shard_map/all_to_all | solution.py:41
  53.3 0.0 copy-done
  53.3 0.1 dynamic-slice_bitcast_fusion.gain
  53.4 1.8 %stage.3.staged = bf16[11776,128]{1,0:T(8,128)(2,1)S(1)} custom-call(bf16[32,16,128]{2,1,0:T(8,128)(2,1)} %merge.1.after, bf16[16384,128]{1,0:T(8,128)(2,1)} %whole_table.1), custom_call_target="tpu_custom_call" | custom-call | bytes 6029312 | tf_op jit(solution)/shard_map/stage/pallas_call | solution.py:102
  55.2 7.5 %all-to-all-done.3.parts = bf16[32,16,128]{2,1,0:T(8,128)(2,1)S(1)} async-done(((bf16[32,16,128]{2,1,0:T(8,128)(2,1)}), bf16[32,16,128]{2,1,0:T(8,128)(2,1)S(1)}, u32[]{:S(2)}, u32[]{:S(2)}) %all-to-all-start.3) | async-done | bytes 131104 | tf_op jit(solution)/shard_map/all_to_all | solution.py:41
  62.7 1.7 %head.1 = (bf16[16,128]{1,0:T(8,128)(2,1)S(1)}, bf16[32,16,512]{2,1,0:T(8,128)(2,1)S(1)}) custom-call(bf16[32,16,128]{2,1,0:T(8,128)(2,1)S(1)} %all-to-all-done.3.parts, bf16[16,128]{1,0:T(8,128)(2,1)S(1)} %reduce_sum.12.after.embedded, f32[1,128]{1,0:T(1,128)S(1)} %dynamic-slice_bitcast_fusion.gain, bf16[11776,128]{1,0:T(8,128)(2,1)S(1)} %stage.3.staged, ...), custom_call_target="tpu_custom_call" | custom-call | tf_op jit(solution)/shard_map/head/pallas_call | solution.py:382
  64.4 18.3 %all_to_all.31.parts = bf16[32,16,512]{2,1,0:T(8,128)(2,1)S(1)} all-to-all(bf16[32,16,512]{2,1,0:T(8,128)(2,1)S(1)} %get-tuple-element.12), channel_id=1, replica_groups=mesh['seq_0'=4,'seq_1'=2,'tensor_0'=4,'tensor_1'=8] {'tensor_1','tensor_0'}, dimensions={0} | all-to-all | bytes 1048576 | tf_op jit(solution)/shard_map/all_to_all | solution.py:41
  82.7 1.0 share.1
  83.7 9.2 %all-to-all-start.5 = ((f32[256,1,128]{2,1,0:T(1,128)}), f32[256,1,128]{2,1,0:T(1,128)S(1)}, u32[]{:S(2)}, u32[]{:S(2)}) async-start(f32[256,1,128]{2,1,0:T(1,128)} %bitcast.6), calls=%async_computation.5 | async-start | bytes 262144 | tf_op jit(solution)/shard_map/all_to_all | solution.py:41
  92.9 0.6 copy.20
  93.5 0.6 copy.19
  94.1 11.8 %all-to-all-done.5 = f32[256,1,128]{2,1,0:T(1,128)S(1)} async-done(((f32[256,1,128]{2,1,0:T(1,128)}), f32[256,1,128]{2,1,0:T(1,128)S(1)}, u32[]{:S(2)}, u32[]{:S(2)}) %all-to-all-start.5) | async-done | bytes 131104 | tf_op jit(solution)/shard_map/all_to_all | solution.py:41
  105.9 0.8 finish.1
  (5 shorter events, 0.0 us)
Async XLA Ops:
  0.6 52.7 %copy-start = (f32[4096]{0:T(1024)S(1)}, f32[4096]{0:T(1024)}, u32[]{:S(2)}) copy-start(f32[4096]{0:T(1024)} %param.13) | copy-start | bytes 49156
  0.6 9.2 %copy-start.3 = (s32[7]{0:T(128)S(1)}, s32[7]{0:T(128)}, u32[]{:S(2)}) copy-start(s32[7]{0:T(128)} %lengths.1) | copy-start | bytes 88
  3.4 31.8 %copy-start.2 = (f32[4096]{0:T(1024)S(1)}, f32[4096]{0:T(1024)}, u32[]{:S(2)}) copy-start(f32[4096]{0:T(1024)} %param.12) | copy-start | bytes 49156
  3.4 11.2 %all-to-all-start = ((bf16[8,16,128]{2,1,0:T(8,128)(2,1)}), bf16[8,16,128]{2,1,0:T(8,128)(2,1)S(1)}, u32[]{:S(2)}, u32[]{:S(2)}) async-start(bf16[8,16,128]{2,1,0:T(8,128)(2,1)} %pick.1), calls=%async_computation | async-start | bytes 65536 | tf_op jit(solution)/shard_map/all_to_all | solution.py:41
  15.3 19.9 %all-to-all-start.1 = ((bf16[32,16,128]{2,1,0:T(8,128)(2,1)}), bf16[32,16,128]{2,1,0:T(8,128)(2,1)S(1)}, u32[]{:S(2)}, u32[]{:S(2)}) async-start(bf16[32,16,128]{2,1,0:T(8,128)(2,1)} %broadcast_in_dim.2), calls=%async_computation.1 | async-start | bytes 262144 | tf_op jit(solution)/shard_map/all_to_all | solution.py:41
  35.2 13.3 %copy-start.1 = (bf16[128,4096]{1,0:T(8,128)(2,1)S(1)}, bf16[128,4096]{1,0:T(8,128)(2,1)}, u32[]{:S(2)}) copy-start(bf16[128,4096]{1,0:T(8,128)(2,1)} %w_out.1) | copy-start | bytes 3145732
  49.4 13.3 %all-to-all-start.3 = ((bf16[32,16,128]{2,1,0:T(8,128)(2,1)}), bf16[32,16,128]{2,1,0:T(8,128)(2,1)S(1)}, u32[]{:S(2)}, u32[]{:S(2)}) async-start(bf16[32,16,128]{2,1,0:T(8,128)(2,1)} %merge.1.after), calls=%async_computation.3 | async-start | bytes 262144 | tf_op jit(solution)/shard_map/all_to_all | solution.py:41
  83.7 22.2 %all-to-all-start.5 = ((f32[256,1,128]{2,1,0:T(1,128)}), f32[256,1,128]{2,1,0:T(1,128)S(1)}, u32[]{:S(2)}, u32[]{:S(2)}) async-start(f32[256,1,128]{2,1,0:T(1,128)} %bitcast.6), calls=%async_computation.5 | async-start | bytes 262144 | tf_op jit(solution)/shard_map/all_to_all | solution.py:41

commit v7 on v6

--- a/solution.py
+++ b/solution.py
@@ -212,14 +212,13 @@
 
 def merge_kernel(rows, slots_at, parts, w_out, out):
     count = parts.shape[0]
-    peaks = [as_column(parts[k, TILE - 2 : TILE - 1, :]) for k in range(count)]
-    highest = functools.reduce(jnp.maximum, peaks)
+    peaks = jnp.concatenate([parts[k, TILE - 2 : TILE - 1, :] for k in range(count)], 0)
+    sums = jnp.concatenate([parts[k, TILE - 1 : TILE, :] for k in range(count)], 0)
+    scales = jnp.exp(peaks - jnp.max(peaks, 0, keepdims=True))
+    denominator = as_column(jnp.sum(sums * scales, 0, keepdims=True))
     numerator = jnp.zeros((TILE, HD), f32)
-    denominator = jnp.zeros((TILE, 1), f32)
     for k in range(count):
-        scale = jnp.exp(peaks[k] - highest)
-        numerator = numerator + parts[k] * scale
-        denominator = denominator + as_column(parts[k, TILE - 1 : TILE, :]) * scale
+        numerator = numerator + parts[k] * as_column(scales[k : k + 1, :])
     real = row_of() < rows
     attended = jnp.where(real, numerator / jnp.where(real, denominator, 1.0), 0.0).astype(bf16)
     per = 8

time: 107 us -> 107 us (level)
  no operation moved by 1% of the time
where the time goes in v7:
time: 107 us
  waiting for transfers between devices  31.4 us (29%)
  starting transfers between devices  30.1 us (28%)
  blocking collectives  27.6 us (26%)
  Pallas kernels  14.5 us (14%)
  local copies, waits for them, and re-layouts  2.05 us (2%)
    all_to_all x4, waiting for transfers between devices, exchange(): return lax.all_to_all(copies, axis, split_axis=0, concat_axis=0, tiled=True)  31.4 us
    all_to_all x4, starting transfers between devices, exchange(): return lax.all_to_all(copies, axis, split_axis=0, concat_axis=0, tiled=True)  30.1 us
    all_to_all x2, blocking collectives, exchange(): return lax.all_to_all(copies, axis, split_axis=0, concat_axis=0, tiled=True)  27.6 us
    pallas_call x1, Pallas kernels, body(): pl.pallas_call(functools.partial(attend_kernel, slots_at), out_shape=(sha...  3.87 us
    pallas_call x2, Pallas kernels, staged(): pl.pallas_call(stage_kernel, out_shape=jax.ShapeDtypeStruct(shape, source...  3.4 us
    pallas_call x1, Pallas kernels, body(): pl.pallas_call(pick_kernel, out_shape=shape((seqs, TILE, HD), bf16), in_s...  2.63 us
  transfers between devices with their start and end apart: 4, of which 4 were waited for; matrix products, arithmetic and copies ran while one was open for 1% of the time, Pallas kernels for 3%

profile of v7, /device:TPU:1, one launch (start us, length us, event | category | flops | bytes accessed | tf_op | source)
XLA Modules:
  0.0 106.7 jit_solution(252273578943883151)
XLA Ops:
  0.6 0.0 copy-start
  0.6 0.0 copy-start.3
  0.7 2.6 %pick.1 = bf16[8,16,128]{2,1,0:T(8,128)(2,1)} custom-call(s32[1]{0:T(128)} %bitcast.place, s32[2,7]{1,0:T(2,128)} %ids.1, bf16[16384,128]{1,0:T(8,128)(2,1)} %whole_table.1), custom_call_target="tpu_custom_call" | custom-call | bytes 131072 | tf_op jit(solution)/shard_map/pick/pallas_call | solution.py:318
  3.3 0.0 copy-start.2
  3.3 6.6 %all-to-all-start = ((bf16[8,16,128]{2,1,0:T(8,128)(2,1)}), bf16[8,16,128]{2,1,0:T(8,128)(2,1)S(1)}, u32[]{:S(2)}, u32[]{:S(2)}) async-start(bf16[8,16,128]{2,1,0:T(8,128)(2,1)} %pick.1), calls=%async_computation | async-start | bytes 65536 | tf_op jit(solution)/shard_map/all_to_all | solution.py:41
  9.9 0.0 copy-done.3
  9.9 0.1 convert_element_type.16
  10.0 4.6 %all-to-all-done = bf16[8,16,128]{2,1,0:T(8,128)(2,1)S(1)} async-done(((bf16[8,16,128]{2,1,0:T(8,128)(2,1)}), bf16[8,16,128]{2,1,0:T(8,128)(2,1)S(1)}, u32[]{:S(2)}, u32[]{:S(2)}) %all-to-all-start) | async-done | bytes 32800 | tf_op jit(solution)/shard_map/all_to_all | solution.py:41
  14.6 0.7 broadcast_in_dim.2
  15.3 10.5 %all-to-all-start.1 = ((bf16[32,16,128]{2,1,0:T(8,128)(2,1)}), bf16[32,16,128]{2,1,0:T(8,128)(2,1)S(1)}, u32[]{:S(2)}, u32[]{:S(2)}) async-start(bf16[32,16,128]{2,1,0:T(8,128)(2,1)} %broadcast_in_dim.2), calls=%async_computation.1 | async-start | bytes 262144 | tf_op jit(solution)/shard_map/all_to_all | solution.py:41
  25.8 0.1 fusion
  26.0 0.1 select_maximum_fusion
  26.1 1.6 %stage.2.w_start = bf16[3,2816,128]{2,1,0:T(8,128)(2,1)S(1)} custom-call(bf16[16,128]{1,0:T(8,128)(2,1)S(1)} %reduce_sum.12.after.embedded, bf16[3,4096,128]{2,1,0:T(8,128)(2,1)} %bitcast.17), custom_call_target="tpu_custom_call" | custom-call | bytes 4325376 | tf_op jit(solution)/shard_map/stage/pallas_call | solution.py:102
  27.6 7.6 %all-to-all-done.1.gathered = bf16[32,16,128]{2,1,0:T(8,128)(2,1)S(1)} async-done(((bf16[32,16,128]{2,1,0:T(8,128)(2,1)}), bf16[32,16,128]{2,1,0:T(8,128)(2,1)S(1)}, u32[]{:S(2)}, u32[]{:S(2)}) %all-to-all-start.1) | async-done | bytes 131104 | tf_op jit(solution)/shard_map/all_to_all | solution.py:41
  35.2 0.0 copy-done.2
  35.2 0.0 copy-start.1
  35.2 3.9 %attend.1 = (f32[8,16,128]{2,1,0:T(8,128)S(1)}, bf16[2,16,128]{2,1,0:T(8,128)(2,1)S(1)}) custom-call(s32[1]{0:T(128)} %bitcast.place, s32[7]{0:T(128)S(1)} %copy-done.3, bf16[32,16,128]{2,1,0:T(8,128)(2,1)S(1)} %all-to-all-done.1.gathered, f32[32,128]{1,0:T(8,128)S(1)} %bitcast.14, f32[16,128]{1,0:T(8,128)S(1)} %get-tuple-element.28.cosine, ...), custom_call_target="tpu_custom_call" | custom-call | tf_op jit(solution)/shard_map/attend/pallas_call | solution.py:345
  39.1 9.4 %all_to_all.30.parts = f32[8,16,128]{2,1,0:T(8,128)S(1)} all-to-all(f32[8,16,128]{2,1,0:T(8,128)S(1)} %get-tuple-element.9), channel_id=1, replica_groups=mesh['seq_0'=4,'seq_1'=2,'tensor_0'=4,'tensor_1'=8] {'seq_0','seq_1'}, dimensions={0} | all-to-all | bytes 131072 | tf_op jit(solution)/shard_map/all_to_all | solution.py:41
  48.5 0.0 copy-done.1
  48.5 1.0 merge.1.after
  49.5 3.9 %all-to-all-start.3 = ((bf16[32,16,128]{2,1,0:T(8,128)(2,1)}), bf16[32,16,128]{2,1,0:T(8,128)(2,1)S(1)}, u32[]{:S(2)}, u32[]{:S(2)}) async-start(bf16[32,16,128]{2,1,0:T(8,128)(2,1)} %merge.1.after), calls=%async_computation.3 | async-start | bytes 262144 | tf_op jit(solution)/shard_map/all_to_all | solution.py:41
  53.3 0.0 copy-done
  53.3 0.1 dynamic-slice_bitcast_fusion.gain
  53.4 1.8 %stage.3.staged = bf16[11776,128]{1,0:T(8,128)(2,1)S(1)} custom-call(bf16[32,16,128]{2,1,0:T(8,128)(2,1)} %merge.1.after, bf16[16384,128]{1,0:T(8,128)(2,1)} %whole_table.1), custom_call_target="tpu_custom_call" | custom-call | bytes 6029312 | tf_op jit(solution)/shard_map/stage/pallas_call | solution.py:102
  55.3 7.5 %all-to-all-done.3.parts = bf16[32,16,128]{2,1,0:T(8,128)(2,1)S(1)} async-done(((bf16[32,16,128]{2,1,0:T(8,128)(2,1)}), bf16[32,16,128]{2,1,0:T(8,128)(2,1)S(1)}, u32[]{:S(2)}, u32[]{:S(2)}) %all-to-all-start.3) | async-done | bytes 131104 | tf_op jit(solution)/shard_map/all_to_all | solution.py:41
  62.7 1.7 %head.1 = (bf16[16,128]{1,0:T(8,128)(2,1)S(1)}, bf16[32,16,512]{2,1,0:T(8,128)(2,1)S(1)}) custom-call(bf16[32,16,128]{2,1,0:T(8,128)(2,1)S(1)} %all-to-all-done.3.parts, bf16[16,128]{1,0:T(8,128)(2,1)S(1)} %reduce_sum.12.after.embedded, f32[1,128]{1,0:T(1,128)S(1)} %dynamic-slice_bitcast_fusion.gain, bf16[11776,128]{1,0:T(8,128)(2,1)S(1)} %stage.3.staged, ...), custom_call_target="tpu_custom_call" | custom-call | tf_op jit(solution)/shard_map/head/pallas_call | solution.py:381
  64.5 18.3 %all_to_all.31.parts = bf16[32,16,512]{2,1,0:T(8,128)(2,1)S(1)} all-to-all(bf16[32,16,512]{2,1,0:T(8,128)(2,1)S(1)} %get-tuple-element.12), channel_id=1, replica_groups=mesh['seq_0'=4,'seq_1'=2,'tensor_0'=4,'tensor_1'=8] {'tensor_1','tensor_0'}, dimensions={0} | all-to-all | bytes 1048576 | tf_op jit(solution)/shard_map/all_to_all | solution.py:41
  82.7 1.0 share.1
  83.8 9.2 %all-to-all-start.5 = ((f32[256,1,128]{2,1,0:T(1,128)}), f32[256,1,128]{2,1,0:T(1,128)S(1)}, u32[]{:S(2)}, u32[]{:S(2)}) async-start(f32[256,1,128]{2,1,0:T(1,128)} %bitcast.6), calls=%async_computation.5 | async-start | bytes 262144 | tf_op jit(solution)/shard_map/all_to_all | solution.py:41
  93.0 0.6 copy.20
  93.6 0.6 copy.19
  94.1 11.8 %all-to-all-done.5 = f32[256,1,128]{2,1,0:T(1,128)S(1)} async-done(((f32[256,1,128]{2,1,0:T(1,128)}), f32[256,1,128]{2,1,0:T(1,128)S(1)}, u32[]{:S(2)}, u32[]{:S(2)}) %all-to-all-start.5) | async-done | bytes 131104 | tf_op jit(solution)/shard_map/all_to_all | solution.py:41
  105.9 0.8 finish.1
  (5 shorter events, 0.0 us)
Async XLA Ops:
  0.6 52.7 %copy-start = (f32[4096]{0:T(1024)S(1)}, f32[4096]{0:T(1024)}, u32[]{:S(2)}) copy-start(f32[4096]{0:T(1024)} %param.13) | copy-start | bytes 49156
  0.6 9.2 %copy-start.3 = (s32[7]{0:T(128)S(1)}, s32[7]{0:T(128)}, u32[]{:S(2)}) copy-start(s32[7]{0:T(128)} %lengths.1) | copy-start | bytes 88
  3.3 31.9 %copy-start.2 = (f32[4096]{0:T(1024)S(1)}, f32[4096]{0:T(1024)}, u32[]{:S(2)}) copy-start(f32[4096]{0:T(1024)} %param.12) | copy-start | bytes 49156
  3.3 11.3 %all-to-all-start = ((bf16[8,16,128]{2,1,0:T(8,128)(2,1)}), bf16[8,16,128]{2,1,0:T(8,128)(2,1)S(1)}, u32[]{:S(2)}, u32[]{:S(2)}) async-start(bf16[8,16,128]{2,1,0:T(8,128)(2,1)} %pick.1), calls=%async_computation | async-start | bytes 65536 | tf_op jit(solution)/shard_map/all_to_all | solution.py:41
  15.3 19.9 %all-to-all-start.1 = ((bf16[32,16,128]{2,1,0:T(8,128)(2,1)}), bf16[32,16,128]{2,1,0:T(8,128)(2,1)S(1)}, u32[]{:S(2)}, u32[]{:S(2)}) async-start(bf16[32,16,128]{2,1,0:T(8,128)(2,1)} %broadcast_in_dim.2), calls=%async_computation.1 | async-start | bytes 262144 | tf_op jit(solution)/shard_map/all_to_all | solution.py:41
  35.2 13.3 %copy-start.1 = (bf16[128,4096]{1,0:T(8,128)(2,1)S(1)}, bf16[128,4096]{1,0:T(8,128)(2,1)}, u32[]{:S(2)}) copy-start(bf16[128,4096]{1,0:T(8,128)(2,1)} %w_out.1) | copy-start | bytes 3145732
  49.5 13.3 %all-to-all-start.3 = ((bf16[32,16,128]{2,1,0:T(8,128)(2,1)}), bf16[32,16,128]{2,1,0:T(8,128)(2,1)S(1)}, u32[]{:S(2)}, u32[]{:S(2)}) async-start(bf16[32,16,128]{2,1,0:T(8,128)(2,1)} %merge.1.after), calls=%async_computation.3 | async-start | bytes 262144 | tf_op jit(solution)/shard_map/all_to_all | solution.py:41
  83.8 22.2 %all-to-all-start.5 = ((f32[256,1,128]{2,1,0:T(1,128)}), f32[256,1,128]{2,1,0:T(1,128)S(1)}, u32[]{:S(2)}, u32[]{:S(2)}) async-start(f32[256,1,128]{2,1,0:T(1,128)} %bitcast.6), calls=%async_computation.5 | async-start | bytes 262144 | tf_op jit(solution)/shard_map/all_to_all | solution.py:41
